TPU v7x, 32 devices: a whole 2x2x4 slice. The times are simulated.
32 devices in a mesh: dx: 16 (over z, x, core), dy: 2 (over y).
Axes of the slice: x: 2, y: 2, z: 4, core: 2. Of those that a mesh axis runs over, the one named last changes fastest.
Arguments:
- img_emb: bfloat16 [16384, 1152], P(('dx', 'dy')), may hold values from -0.1796875 to 0.1796875
- txt_emb: bfloat16 [16384, 1152], P(('dx', 'dy')), may hold values from -0.1796875 to 0.1796875
- logit_scale: float32 [1], replicated, may hold values from 4 to 8
- logit_bias: float32 [1], replicated, may hold values from -3 to -1
Outputs:
- grad_img: float32 [16384, 1152], P(('dx', 'dy'))
- grad_txt: float32 [16384, 1152], P(('dx', 'dy'))
All inputs are finite; a program needn't handle non-finite values.
Results may differ from a plain program's by a relative error of at most 0.0049.
Values may be sent and summed in bfloat16 or wider, within the bound.
No kernel may reach another device: no remote copies, remote signals or barrier semaphores. Data moves between devices by JAX's collectives and lax.ppermute only.
A program may use at most 64 MiB of HBM per device.

v0:
```python
import jax
import jax.numpy as jnp
from jax import lax
from jax.sharding import PartitionSpec as P


def from_partner(value, axis, stride):
    return lax.ppermute(value, axis, [(i, i ^ 1 << stride) for i in range(lax.axis_size(axis))])


def normalize(values):
    floats = values.astype(jnp.float32)
    inverse = lax.rsqrt(jnp.sum(floats * floats, axis=-1, keepdims=True) + 1e-06)
    return (floats * inverse, inverse)


def tile_weights(images, texts, scale, bias, diagonal):
    logits = (
        scale
        * lax.dot_general(
            images, texts, (((1,), (1,)), ((), ())), preferred_element_type=jnp.float32
        )
        + bias
    )
    if diagonal:
        eye = jnp.arange(images.shape[0])[:, None] == jnp.arange(texts.shape[0])[None, :]
        signs = jnp.where(eye, jnp.float32(1.0), jnp.float32(-1.0))
    else:
        signs = jnp.full(logits.shape, -1.0, jnp.float32)
    coeffs = -signs * jax.nn.sigmoid(-signs * logits)
    return (scale * coeffs).astype(jnp.bfloat16)


def transposed(coeffs, images):
    return lax.dot_general(
        coeffs, images, (((0,), (0,)), ((), ())), preferred_element_type=jnp.float32
    )


def finish(unit, inverse, grads):
    return inverse * (grads - unit * jnp.sum(unit * grads, axis=-1, keepdims=True))


def per_device(img_emb, txt_emb, logit_scale, logit_bias):
    img_unit, inv_img = normalize(img_emb)
    txt_unit, inv_txt = normalize(txt_emb)
    img_b = img_unit.astype(jnp.bfloat16)
    txt_b = txt_unit.astype(jnp.bfloat16)
    scale = logit_scale[0]
    bias = logit_bias[0]
    own_coeffs = tile_weights(img_b, txt_b, scale, bias, True)
    grad_i = jnp.dot(own_coeffs, txt_b, preferred_element_type=jnp.float32)
    grad_t = transposed(own_coeffs, img_b)
    top_bit = lax.axis_size("dx").bit_length() - 2

    def forward_part(far_txt):
        coeffs = tile_weights(img_b, far_txt, scale, bias, False)
        more = jnp.dot(coeffs, far_txt, preferred_element_type=jnp.float32)
        return (more, transposed(coeffs, img_b).astype(jnp.bfloat16))

    far_txt = from_partner(txt_b, "dy", 0)
    more, partial_value = forward_part(far_txt)
    grad_i = grad_i + more
    grad_t = grad_t + from_partner(partial_value, "dy", 0).astype(jnp.float32)
    for bit_index in (0, top_bit, 1):
        far_txt = from_partner(txt_b, "dx", bit_index)
        more, partial_value = forward_part(far_txt)
        grad_i = grad_i + more
        grad_t = grad_t + from_partner(partial_value, "dx", bit_index).astype(jnp.float32)
    return (finish(img_unit, inv_img, grad_i), finish(txt_unit, inv_txt, grad_t))


def solution(mesh):
    return jax.shard_map(
        per_device,
        mesh=mesh,
        in_specs=(P(("dx", "dy"), None), P(("dx", "dy"), None), P(), P()),
        out_specs=(P(("dx", "dy"), None), P(("dx", "dy"), None)),
        check_vma=False,
    )
```

profile of v0, /device:TPU:0, one launch (start us, length us, event | category | flops | bytes accessed | tf_op | source)
XLA Modules:
  0.0 118.5 jit_solution(10397629900931139057)
XLA Ops:
  0.6 0.0 copy-start
  0.6 1.7 %fusion.15 = f32[512]{0:T(512)S(1)} fusion(bf16[512,1152]{1,0:T(8,128)(2,1)} %param.5), kind=kLoop, calls=%fused_computation.25 | loop fusion | flops 1768960 | bytes 1181696 | tf_op jit(solution)/shard_map/reduce_sum | solution.py:13
  2.3 0.0 copy-done
  2.3 0.0 copy-start.1
  2.3 0.3 fusion.4
  2.6 3.0 %collective-permute-start.3 = (bf16[512,1152]{1,0:T(8,128)(2,1)S(1)}, bf16[512,1152]{1,0:T(8,128)(2,1)S(1)}, u32[]{:S(2)}, u32[]{:S(2)}) collective-permute-start(bf16[512,1152]{1,0:T(8,128)(2,1)S(1)} %fusion.4), channel_id=1, source_target_pairs={{0,4},{2,6},{4,0},{6,2},{8,12},{10,14},{12,8},{14,10},{16,20},{18,... | collective-permute-start | bytes 3538952 | tf_op jit(solution)/shard_map/ppermute | solution.py:8
  5.6 2.6 %collective-permute-start.2 = (bf16[512,1152]{1,0:T(8,128)(2,1)S(1)}, bf16[512,1152]{1,0:T(8,128)(2,1)S(1)}, u32[]{:S(2)}, u32[]{:S(2)}) collective-permute-start(bf16[512,1152]{1,0:T(8,128)(2,1)S(1)} %fusion.4), channel_id=1, source_target_pairs={{0,16},{2,18},{4,20},{6,22},{8,24},{10,26},{12,28},{14,30},{16,0},... | collective-permute-start | bytes 3538952 | tf_op jit(solution)/shard_map/ppermute | solution.py:8
  8.2 1.5 %collective-permute-start = (bf16[512,1152]{1,0:T(8,128)(2,1)S(1)}, bf16[512,1152]{1,0:T(8,128)(2,1)S(1)}, u32[]{:S(2)}, u32[]{:S(2)}) collective-permute-start(bf16[512,1152]{1,0:T(8,128)(2,1)S(1)} %fusion.4), channel_id=1, source_target_pairs={{0,1},{1,0},{2,3},{3,2},{4,5},{5,4},{6,7},{7,6},{8,9},{9,8},{10,11... | collective-permute-start | bytes 3538952 | tf_op jit(solution)/shard_map/ppermute | solution.py:8
  9.7 0.0 collective-permute-start.1
  11.0 0.0 copy-done.1
  11.0 0.3 fusion.11
  11.3 1.1 fusion.48
  12.5 0.8 fusion.64
  13.3 18.3 %collective-permute-done.3 = bf16[512,1152]{1,0:T(8,128)(2,1)S(1)} collective-permute-done((bf16[512,1152]{1,0:T(8,128)(2,1)S(1)}, bf16[512,1152]{1,0:T(8,128)(2,1)S(1)}, u32[]{:S(2)}, u32[]{:S(2)}) %collective-permute-start.3) | collective-permute-done | bytes 1179680 | tf_op jit(solution)/shard_map/ppermute | solution.py:8
  31.6 1.1 fusion.49
  32.6 1.0 convolution_convert_fusion
  33.6 1.8 %collective-permute-start.7 = (bf16[512,1152]{1,0:T(8,128)(2,1)S(1)}, bf16[512,1152]{1,0:T(8,128)(2,1)S(1)}, u32[]{:S(2)}, u32[]{:S(2)}) collective-permute-start(bf16[512,1152]{1,0:T(8,128)(2,1)S(1)} %convolution_convert_fusion), channel_id=1, source_target_pairs={{0,4},{2,6},{4,0},{6,2},{8,12},{10,14},{12,8},{14,10},{16,20},{18,... | collective-permute-start | bytes 3538952 | tf_op jit(solution)/shard_map/ppermute | solution.py:8
  35.4 23.8 %collective-permute-done.2 = bf16[512,1152]{1,0:T(8,128)(2,1)S(1)} collective-permute-done((bf16[512,1152]{1,0:T(8,128)(2,1)S(1)}, bf16[512,1152]{1,0:T(8,128)(2,1)S(1)}, u32[]{:S(2)}, u32[]{:S(2)}) %collective-permute-start.2) | collective-permute-done | bytes 1179680 | tf_op jit(solution)/shard_map/ppermute | solution.py:8
  59.2 1.1 fusion.50
  60.3 0.9 convolution_convert_fusion.1
  61.2 0.1 collective-permute-start.6
  61.3 0.0 collective-permute-done.1
  61.3 1.1 fusion.51
  62.4 1.0 convolution_convert_fusion.2
  63.4 0.1 collective-permute-start.5
  63.4 0.0 collective-permute-done
  63.4 1.1 fusion.52
  64.5 0.9 convolution_convert_fusion.3
  65.5 1.6 %collective-permute-start.4 = (bf16[512,1152]{1,0:T(8,128)(2,1)S(1)}, bf16[512,1152]{1,0:T(8,128)(2,1)S(1)}, u32[]{:S(2)}, u32[]{:S(2)}) collective-permute-start(bf16[512,1152]{1,0:T(8,128)(2,1)S(1)} %convolution_convert_fusion.3), channel_id=1, source_target_pairs={{0,1},{1,0},{2,3},{3,2},{4,5},{5,4},{6,7},{7,6},{8,9},{9,8},{10,11... | collective-permute-start | bytes 3538952 | tf_op jit(solution)/shard_map/ppermute | solution.py:8
  67.0 0.8 fusion.66
  67.9 0.8 fusion.65
  68.7 0.8 convolution_add_fusion.1
  69.6 1.5 %fusion.8 = (f32[512]{0:T(512)S(1)}, f32[512,1152]{1,0:T(8,128)S(1)}) fusion(bf16[512,1152]{1,0:T(8,128)(2,1)S(1)} %copy-done.1, f32[512]{0:T(512)S(1)} %add_rsqrt_fusion.1, f32[512,1152]{1,0:T(8,128)S(1)} %fusion.66, f32[512,1152]{1,0:T(8,128)S(1)} %fusion.65, f32[512,1152]{1,0:T(8,128)S(1)} %convolution_add_fusion.1, bf16[512,512]{1,0:T(8,128)(2,1)S(1)} %fusion.51, ...), kind=kOutput, calls=%fused_computation.18 | convolution fusion | flops 608108032 | bytes 12324864 | tf_op jit(solution)/shard_map/dot_general | solution.py:58
  71.1 1.9 %fusion.10 = f32[512,1152]{1,0:T(8,128)} fusion(f32[512,1152]{1,0:T(8,128)S(1)} %get-tuple-element.3, bf16[512,1152]{1,0:T(8,128)(2,1)S(1)} %copy-done.1, f32[512]{0:T(512)S(1)} %get-tuple-element.2, f32[512]{0:T(512)S(1)} %add_rsqrt_fusion.1), kind=kLoop, calls=%fused_computation.20 | loop fusion | flops 2949120 | bytes 5902336 | tf_op jit(solution)/shard_map/mul | solution.py:41
  73.0 0.0 collective-permute-done.7
  73.0 41.4 %collective-permute-done.6 = bf16[512,1152]{1,0:T(8,128)(2,1)S(1)} collective-permute-done((bf16[512,1152]{1,0:T(8,128)(2,1)S(1)}, bf16[512,1152]{1,0:T(8,128)(2,1)S(1)}, u32[]{:S(2)}, u32[]{:S(2)}) %collective-permute-start.6) | collective-permute-done | bytes 1179680 | tf_op jit(solution)/shard_map/ppermute | solution.py:8
  114.3 0.0 collective-permute-done.5
  114.3 0.0 collective-permute-done.4
  114.3 1.8 %fusion.12 = (f32[512]{0:T(512)S(1)}, f32[512,1152]{1,0:T(8,128)S(1)}) fusion(bf16[512,1152]{1,0:T(8,128)(2,1)S(1)} %copy-done, f32[512]{0:T(512)S(1)} %add_rsqrt_fusion, bf16[512,1152]{1,0:T(8,128)(2,1)S(1)} %collective-permute-done.7, bf16[512,1152]{1,0:T(8,128)(2,1)S(1)} %collective-permute-done.6, bf16[512,1152]{1,0:T(8,128)(2,1)S(1)} %collective-permute-done.5, ...), kind=kOutput, calls=%fused_computation.22 | convolution fusion | flops 612826624 | bytes 9967616 | tf_op jit(solution)/shard_map/dot_general | solution.py:35
  116.1 2.4 %fusion.14 = f32[512,1152]{1,0:T(8,128)} fusion(bf16[512,1152]{1,0:T(8,128)(2,1)S(1)} %copy-done, f32[512]{0:T(512)S(1)} %get-tuple-element.4, f32[512]{0:T(512)S(1)} %add_rsqrt_fusion, bf16[512,1152]{1,0:T(8,128)(2,1)S(1)} %collective-permute-done.7, bf16[512,1152]{1,0:T(8,128)(2,1)S(1)} %collective-permute-done.6, ...), kind=kLoop, calls=%fused_computation.24 | loop fusion | flops 7667712 | bytes 10620928 | tf_op jit(solution)/shard_map/mul | solution.py:41
  (2 shorter events, 0.0 us)
Async XLA Ops:
  0.6 1.7 %copy-start = (bf16[512,1152]{1,0:T(8,128)(2,1)S(1)}, bf16[512,1152]{1,0:T(8,128)(2,1)}, u32[]{:S(2)}) copy-start(bf16[512,1152]{1,0:T(8,128)(2,1)} %param.5) | copy-start | bytes 3538948
  2.3 8.7 %copy-start.1 = (bf16[512,1152]{1,0:T(8,128)(2,1)S(1)}, bf16[512,1152]{1,0:T(8,128)(2,1)}, u32[]{:S(2)}) copy-start(bf16[512,1152]{1,0:T(8,128)(2,1)} %param.4) | copy-start | bytes 3538948
  2.6 29.0 %collective-permute-start.3 = (bf16[512,1152]{1,0:T(8,128)(2,1)S(1)}, bf16[512,1152]{1,0:T(8,128)(2,1)S(1)}, u32[]{:S(2)}, u32[]{:S(2)}) collective-permute-start(bf16[512,1152]{1,0:T(8,128)(2,1)S(1)} %fusion.4), channel_id=1, source_target_pairs={{0,4},{2,6},{4,0},{6,2},{8,12},{10,14},{12,8},{14,10},{16,20},{18,... | collective-permute-start | bytes 3538952 | tf_op jit(solution)/shard_map/ppermute | solution.py:8
  5.6 53.6 %collective-permute-start.2 = (bf16[512,1152]{1,0:T(8,128)(2,1)S(1)}, bf16[512,1152]{1,0:T(8,128)(2,1)S(1)}, u32[]{:S(2)}, u32[]{:S(2)}) collective-permute-start(bf16[512,1152]{1,0:T(8,128)(2,1)S(1)} %fusion.4), channel_id=1, source_target_pairs={{0,16},{2,18},{4,20},{6,22},{8,24},{10,26},{12,28},{14,30},{16,0},... | collective-permute-start | bytes 3538952 | tf_op jit(solution)/shard_map/ppermute | solution.py:8
  8.2 55.2 %collective-permute-start = (bf16[512,1152]{1,0:T(8,128)(2,1)S(1)}, bf16[512,1152]{1,0:T(8,128)(2,1)S(1)}, u32[]{:S(2)}, u32[]{:S(2)}) collective-permute-start(bf16[512,1152]{1,0:T(8,128)(2,1)S(1)} %fusion.4), channel_id=1, source_target_pairs={{0,1},{1,0},{2,3},{3,2},{4,5},{5,4},{6,7},{7,6},{8,9},{9,8},{10,11... | collective-permute-start | bytes 3538952 | tf_op jit(solution)/shard_map/ppermute | solution.py:8
  9.7 51.6 %collective-permute-start.1 = (bf16[512,1152]{1,0:T(8,128)(2,1)S(1)}, bf16[512,1152]{1,0:T(8,128)(2,1)S(1)}, u32[]{:S(2)}, u32[]{:S(2)}) collective-permute-start(bf16[512,1152]{1,0:T(8,128)(2,1)S(1)} %fusion.4), channel_id=1, source_target_pairs={{0,2},{2,0},{4,6},{6,4},{8,10},{10,8},{12,14},{14,12},{16,18},{18,... | collective-permute-start | bytes 3538952 | tf_op jit(solution)/shard_map/ppermute | solution.py:8
  33.6 39.3 %collective-permute-start.7 = (bf16[512,1152]{1,0:T(8,128)(2,1)S(1)}, bf16[512,1152]{1,0:T(8,128)(2,1)S(1)}, u32[]{:S(2)}, u32[]{:S(2)}) collective-permute-start(bf16[512,1152]{1,0:T(8,128)(2,1)S(1)} %convolution_convert_fusion), channel_id=1, source_target_pairs={{0,4},{2,6},{4,0},{6,2},{8,12},{10,14},{12,8},{14,10},{16,20},{18,... | collective-permute-start | bytes 3538952 | tf_op jit(solution)/shard_map/ppermute | solution.py:8
  61.2 53.1 %collective-permute-start.6 = (bf16[512,1152]{1,0:T(8,128)(2,1)S(1)}, bf16[512,1152]{1,0:T(8,128)(2,1)S(1)}, u32[]{:S(2)}, u32[]{:S(2)}) collective-permute-start(bf16[512,1152]{1,0:T(8,128)(2,1)S(1)} %convolution_convert_fusion.1), channel_id=1, source_target_pairs={{0,16},{2,18},{4,20},{6,22},{8,24},{10,26},{12,28},{14,30},{16,0},... | collective-permute-start | bytes 3538952 | tf_op jit(solution)/shard_map/ppermute | solution.py:8
  63.4 51.0 %collective-permute-start.5 = (bf16[512,1152]{1,0:T(8,128)(2,1)S(1)}, bf16[512,1152]{1,0:T(8,128)(2,1)S(1)}, u32[]{:S(2)}, u32[]{:S(2)}) collective-permute-start(bf16[512,1152]{1,0:T(8,128)(2,1)S(1)} %convolution_convert_fusion.2), channel_id=1, source_target_pairs={{0,2},{2,0},{4,6},{6,4},{8,10},{10,8},{12,14},{14,12},{16,18},{18,... | collective-permute-start | bytes 3538952 | tf_op jit(solution)/shard_map/ppermute | solution.py:8
  65.5 48.9 %collective-permute-start.4 = (bf16[512,1152]{1,0:T(8,128)(2,1)S(1)}, bf16[512,1152]{1,0:T(8,128)(2,1)S(1)}, u32[]{:S(2)}, u32[]{:S(2)}) collective-permute-start(bf16[512,1152]{1,0:T(8,128)(2,1)S(1)} %convolution_convert_fusion.3), channel_id=1, source_target_pairs={{0,1},{1,0},{2,3},{3,2},{4,5},{5,4},{6,7},{7,6},{8,9},{9,8},{10,11... | collective-permute-start | bytes 3538952 | tf_op jit(solution)/shard_map/ppermute | solution.py:8
where the time goes:
time: 119 us; the launch traced here: 118 us
  waiting for transfers between devices  83.5 us (70%)
  matrix products  15.7 us (13%)
  starting transfers between devices  10.6 us (9%)
  other arithmetic  6.56 us (6%)
  between operations  2.09 us (2%)
    ppermute x8, waiting for transfers between devices, from_partner(): lax.ppermute(value, axis, [(i, i ^ 1 << stride) for i in range(lax.axis_s...  83.5 us
    ppermute x8, starting transfers between devices, from_partner(): lax.ppermute(value, axis, [(i, i ^ 1 << stride) for i in range(lax.axis_s...  10.6 us
    dot_general x5, matrix products, transposed(): lax.dot_general(coeffs, images, (((0,), (0,)), ((), ())), preferred_eleme...  5.57 us
    dot_general x5, matrix products, tile_weights(): lax.dot_general(images, texts, (((1,), (1,)), ((), ())), preferred_elemen...  5.32 us
    mul x2, other arithmetic, finish(): inverse * (grads - unit * jnp.sum(unit * grads, axis=-1, keepdims=True))  4.31 us
    dot_general x4, matrix products, forward_part(): more = jnp.dot(coeffs, far_txt, preferred_element_type=jnp.float32)  4 us
  transfers between devices with their start and end apart: 8, of which 3 were waited for; matrix products, arithmetic and copies ran while one was open for 14% of the time, Pallas kernels for 0%

commit v1 on v0

--- a/solution.py
+++ b/solution.py
@@ -1,11 +1,80 @@
+import functools
+
 import jax
 import jax.numpy as jnp
 from jax import lax
+from jax.experimental import pallas as pl
+from jax.experimental.pallas import tpu as pltpu
 from jax.sharding import PartitionSpec as P
 
+STEP = 32
 
-def from_partner(value, axis, stride):
-    return lax.ppermute(value, axis, [(i, i ^ 1 << stride) for i in range(lax.axis_size(axis))])
+
+def unit_kernel(*refs):
+    for values, rounded in zip(refs[:2], refs[2:]):
+        floats = values[...].astype(jnp.float32)
+        inverse = lax.rsqrt(jnp.sum(floats * floats, axis=-1, keepdims=True) + 1e-06)
+        rounded[...] = (floats * inverse).astype(jnp.bfloat16)
+
+
+def rounded_units(*arrays):
+    rows, width = arrays[0].shape
+    block = pl.BlockSpec((rows // 4, width), lambda i: (i, 0))
+    shape = jax.ShapeDtypeStruct((rows, width), jnp.bfloat16)
+    return pl.pallas_call(
+        unit_kernel,
+        grid=(4,),
+        out_shape=(shape, shape),
+        in_specs=[block, block],
+        out_specs=(block, block),
+    )(*arrays)
+
+
+def add_kernel(offsets, odd, base, *refs):
+    parts, (out, total, sems) = refs[: len(offsets) + (odd is not None)], refs[-3:]
+    copies = []
+    for index, offset in enumerate(offsets):
+        for at in range(parts[index].shape[0] // STEP):
+            here = pl.ds(at * STEP, STEP)
+            there = pl.ds(offset + at * STEP, STEP)
+            slot = pl.ds(len(copies) * STEP, STEP)
+            part = parts[index][here].astype(jnp.float32)
+            if odd is not None and index == len(offsets) - 1:
+                is_odd = odd(lax.axis_index("dx")) == 1
+                part = jnp.where(is_odd, parts[index + 1][here].astype(jnp.float32), part)
+            total[slot] = base[there] + part
+            copies.append(
+                pltpu.make_async_copy(total.at[slot], out.at[there], sems.at[len(copies)])
+            )
+            copies[-1].start()
+    for copy in copies:
+        copy.wait()
+
+
+def add_rows(base, parts, offsets, out=None, odd=None):
+    vmem, hbm = (pl.BlockSpec(memory_space=space) for space in (pltpu.VMEM, pltpu.HBM))
+    args = [base, *parts] + ([] if out is None else [out])
+    rows = sum(part.shape[0] for part in parts[: len(offsets)])
+    return pl.pallas_call(
+        functools.partial(add_kernel, offsets, odd),
+        out_shape=jax.ShapeDtypeStruct(base.shape, jnp.float32),
+        in_specs=[vmem] * (1 + len(parts)) + ([] if out is None else [hbm]),
+        out_specs=hbm,
+        scratch_shapes=[
+            pltpu.VMEM((rows, base.shape[1]), jnp.float32),
+            pltpu.SemaphoreType.DMA((rows // STEP,)),
+        ],
+        input_output_aliases={} if out is None else {len(args) - 1: 0},
+        compiler_params=pltpu.CompilerParams(vmem_limit_bytes=16 * 2**20),
+        cost_estimate=pl.CostEstimate(
+            flops=rows * base.shape[1], bytes_accessed=10 * rows * base.shape[1], transcendentals=0
+        ),
+    )(*args)
+
+
+def from_partner(value, axis, stride, among=lambda index: True):
+    pairs = [(i, i ^ 1 << stride) for i in range(lax.axis_size(axis)) if among(i)]
+    return lax.ppermute(value, axis, pairs)
 
 
 def normalize(values):
@@ -42,32 +111,77 @@
 
 
 def per_device(img_emb, txt_emb, logit_scale, logit_bias):
-    img_unit, inv_img = normalize(img_emb)
-    txt_unit, inv_txt = normalize(txt_emb)
-    img_b = img_unit.astype(jnp.bfloat16)
-    txt_b = txt_unit.astype(jnp.bfloat16)
+    top_bit = lax.axis_size("dx").bit_length() - 2
+    half = txt_emb.shape[0] // 2
+
+    def odd(index):
+        return index >> (top_bit - 1) & 1
+
+    first, txt_emb, img_emb = lax.optimization_barrier((txt_emb[:half], txt_emb, img_emb))
+    far_raw = [from_partner(first, "dx", top_bit), from_partner(txt_emb[half:], "dx", top_bit)]
+    img_b, txt_b = rounded_units(img_emb, txt_emb)
     scale = logit_scale[0]
     bias = logit_bias[0]
+
     own_coeffs = tile_weights(img_b, txt_b, scale, bias, True)
     grad_i = jnp.dot(own_coeffs, txt_b, preferred_element_type=jnp.float32)
     grad_t = transposed(own_coeffs, img_b)
-    top_bit = lax.axis_size("dx").bit_length() - 2
 
     def forward_part(far_txt):
         coeffs = tile_weights(img_b, far_txt, scale, bias, False)
         more = jnp.dot(coeffs, far_txt, preferred_element_type=jnp.float32)
-        return (more, transposed(coeffs, img_b).astype(jnp.bfloat16))
+        return (more, transposed(coeffs, img_b))
 
-    far_txt = from_partner(txt_b, "dy", 0)
-    more, partial_value = forward_part(far_txt)
+    near = (("dx", 0), ("dy", 0), ("dx", 1))
+    near_b, own_coeffs = lax.optimization_barrier((txt_b, own_coeffs))
+    near_txt = [from_partner(near_b, axis, bit) for axis, bit in near]
+
+    def far_part(raw):
+        far_unit, far_inv = normalize(raw)
+        more, partial_value = forward_part(far_unit.astype(jnp.bfloat16))
+        return (more, finish(far_unit, far_inv, partial_value).astype(jnp.bfloat16))
+
+    more, partial_value = far_part(far_raw[0])
     grad_i = grad_i + more
-    grad_t = grad_t + from_partner(partial_value, "dy", 0).astype(jnp.float32)
-    for bit_index in (0, top_bit, 1):
-        far_txt = from_partner(txt_b, "dx", bit_index)
-        more, partial_value = forward_part(far_txt)
+    far_back = [from_partner(partial_value, "dx", top_bit)]
+    partial_value, near_txt, img_emb, txt_emb = lax.optimization_barrier(
+        (partial_value, near_txt, img_emb, txt_emb)
+    )
+    img_unit, inv_img = normalize(img_emb)
+    txt_unit, inv_txt = normalize(txt_emb)
+
+    near_partials = []
+    for at, (axis, bit) in enumerate(near):
+        more, partial_value = forward_part(near_txt[at])
         grad_i = grad_i + more
-        grad_t = grad_t + from_partner(partial_value, "dx", bit_index).astype(jnp.float32)
-    return (finish(img_unit, inv_img, grad_i), finish(txt_unit, inv_txt, grad_t))
+        near_partials.append(partial_value.astype(jnp.bfloat16))
+
+    near_back = [from_partner(near_partials[0], *near[0])]
+    raw, _, near_back = lax.optimization_barrier((far_raw[1], near_partials, near_back))
+    more, partial_value = far_part(raw)
+    grad_i = grad_i + more
+    most = half * 3 // 8 // STEP * STEP
+    last = half - STEP
+    far_back.append(from_partner(partial_value[:most], "dx", top_bit))
+    far_back.append(from_partner(partial_value[most:last], "dx", top_bit))
+    rest = partial_value[last:]
+    even_back = from_partner(rest, "dx", top_bit, lambda index: not odd(index))
+    for (axis, bit), partial_value in zip(near[1:], near_partials[1:]):
+        near_back.append(from_partner(partial_value, axis, bit))
+    for partial_value in near_back:
+        grad_t = grad_t + partial_value.astype(jnp.float32)
+    grad_img, base, returned = lax.optimization_barrier(
+        (finish(img_unit, inv_img, grad_i), finish(txt_unit, inv_txt, grad_t), far_back[0])
+    )
+    grad_txt = add_rows(base, [returned], (0,))
+    rest, far_back[1], grad_txt, grad_img = lax.optimization_barrier(
+        (rest, far_back[1], grad_txt, grad_img)
+    )
+    odd_back = from_partner(rest, "dx", top_bit, odd)
+    grad_txt = add_rows(base, [far_back[1]], (half,), grad_txt)
+    grad_txt = add_rows(base, [far_back[2]], (half + most,), grad_txt)
+    grad_txt = add_rows(base, [even_back, odd_back], (half + last,), grad_txt, odd)
+    return (grad_img, grad_txt)
 
 
 def solution(mesh):

time: 119 us -> 107 us (0.90)
  waiting for transfers between devices: 83.5 us -> 56.6 us
  Pallas kernels: 0 us -> 7.53 us
  starting transfers between devices: 10.6 us -> 16.8 us
  other arithmetic: 6.56 us -> 4.33 us
  matrix products: 15.7 us -> 17.8 us
  local copies, waits for them, and re-layouts: 0.01 us -> 1.65 us
    ppermute x8 -> x13, waiting for transfers between devices: 83.5 us -> 56.6 us  [from_partner(): return lax.ppermute(value, axis, pairs)]
    pallas_call x0 -> x5, Pallas kernels: none -> 7.53 us  [the longest x1 4.08 us: rounded_units(): pl.pallas_call(unit_kernel, grid=(4,), out_shape=(shape, shape), in_specs...]
    ppermute x8 -> x13, starting transfers between devices: 10.6 us -> 16.8 us  [from_partner(): return lax.ppermute(value, axis, pairs)]
    dot_general x5 -> x6, matrix products: 5.32 us -> 7.22 us  [tile_weights(): lax.dot_general(images, texts, (((1,), (1,)), ((), ())), preferred_elemen...]
    mul x2, other arithmetic: 4.31 us -> 2.73 us  [finish(): inverse * (grads - unit * jnp.sum(unit * grads, axis=-1, keepdims=True))]
    slice x0 -> x5, local copies, waits for them, and re-layouts: none -> 1.21 us  [the longest x1 1.11 us: per_device(): txt_emb[:half]]
    dot_general x4 -> x5, matrix products: 4 us -> 4.32 us  [forward_part(): more = jnp.dot(coeffs, far_txt, preferred_element_type=jnp.float32)]
    dot_general x5 -> x6, matrix products: 5.57 us -> 5.39 us  [transposed(): lax.dot_general(coeffs, images, (((0,), (0,)), ((), ())), preferred_eleme...]
  transfers between devices with their start and end apart: 8 -> 13, of which waited for: 3 -> 7; matrix products, arithmetic and copies ran while one was open for 14% -> 21% of each run, Pallas kernels for 0% -> 6%
where the time goes in v1:
time: 107 us
  waiting for transfers between devices  56.6 us (53%)
  matrix products  17.8 us (17%)
  starting transfers between devices  16.8 us (16%)
  Pallas kernels  7.53 us (7%)
  other arithmetic  4.33 us (4%)
  between operations  2.38 us (2%)
  local copies, waits for them, and re-layouts  1.65 us (2%)
    ppermute x13, waiting for transfers between devices, from_partner(): return lax.ppermute(value, axis, pairs)  56.6 us
    ppermute x13, starting transfers between devices, from_partner(): return lax.ppermute(value, axis, pairs)  16.8 us
    dot_general x6, matrix products, tile_weights(): lax.dot_general(images, texts, (((1,), (1,)), ((), ())), preferred_elemen...  7.22 us
    dot_general x6, matrix products, transposed(): lax.dot_general(coeffs, images, (((0,), (0,)), ((), ())), preferred_eleme...  5.39 us
    dot_general x5, matrix products, forward_part(): more = jnp.dot(coeffs, far_txt, preferred_element_type=jnp.float32)  4.32 us
    pallas_call x1, Pallas kernels, rounded_units(): pl.pallas_call(unit_kernel, grid=(4,), out_shape=(shape, shape), in_specs...  4.08 us
    pallas_call x4, Pallas kernels, add_rows(): pl.pallas_call(functools.partial(add_kernel, offsets, odd), out_shape=jax...  3.45 us
    mul x2, other arithmetic, finish(): inverse * (grads - unit * jnp.sum(unit * grads, axis=-1, keepdims=True))  2.73 us
  transfers between devices with their start and end apart: 13, of which 7 were waited for; matrix products, arithmetic and copies ran while one was open for 21% of the time, Pallas kernels for 6%

profile of v1, /device:TPU:0, one launch (start us, length us, event | category | flops | bytes accessed | tf_op | source)
XLA Modules:
  0.0 107.0 jit_solution(1776861244576564073)
XLA Ops:
  0.6 1.1 %slice.15 = bf16[256,1152]{1,0:T(8,128)(2,1)S(1)} slice(bf16[512,1152]{1,0:T(8,128)(2,1)} %refs_1_), slice={[0:256], [0:1152]} | slice | bytes 1179648 | tf_op jit(solution)/shard_map/slice | solution.py:120
  1.7 4.1 %collective-permute-start.1 = (bf16[256,1152]{1,0:T(8,128)(2,1)S(1)}, bf16[256,1152]{1,0:T(8,128)(2,1)S(1)}, u32[]{:S(2)}, u32[]{:S(2)}) collective-permute-start(bf16[256,1152]{1,0:T(8,128)(2,1)S(1)} %slice.15), channel_id=1, source_target_pairs={{0,16},{2,18},{4,20},{6,22},{8,24},{10,26},{12,28},{14,30},{16,0},... | collective-permute-start | bytes 1769480 | tf_op jit(solution)/shard_map/ppermute | solution.py:77
  7.1 4.1 %shard_map.59 = (bf16[512,1152]{1,0:T(8,128)(2,1)}, bf16[512,1152]{1,0:T(8,128)(2,1)}) custom-call(bf16[512,1152]{1,0:T(8,128)(2,1)} %refs_0_, bf16[512,1152]{1,0:T(8,128)(2,1)} %refs_1_), custom_call_target="tpu_custom_call" | custom-call | tf_op jit(solution)/shard_map/pallas_call | solution.py:24
  11.2 2.8 %fusion.47 = bf16[512,512]{1,0:T(8,128)(2,1)S(1)} fusion(bf16[512,1152]{1,0:T(8,128)(2,1)} %get-tuple-element.24, bf16[512,1152]{1,0:T(8,128)(2,1)} %get-tuple-element.27, f32[]{:T(128)} %bitcast.41, f32[]{:T(128)} %bitcast.38), kind=kOutput, calls=%fused_computation.65 | convolution fusion | flops 607125504 | bytes 2883592 | tf_op jit(solution)/shard_map/dot_general | solution.py:89
  14.2 1.6 %collective-permute-start.3 = (bf16[512,1152]{1,0:T(8,128)(2,1)S(1)}, bf16[512,1152]{1,0:T(8,128)(2,1)S(1)}, u32[]{:S(2)}, u32[]{:S(2)}) collective-permute-start(bf16[512,1152]{1,0:T(8,128)(2,1)S(1)} %copy-done.3), channel_id=1, source_target_pairs={{0,1},{1,0},{2,3},{3,2},{4,5},{5,4},{6,7},{7,6},{8,9},{9,8},{10,11... | collective-permute-start | bytes 3538952 | tf_op jit(solution)/shard_map/ppermute | solution.py:77
  15.7 1.5 %collective-permute-start.4 = (bf16[512,1152]{1,0:T(8,128)(2,1)S(1)}, bf16[512,1152]{1,0:T(8,128)(2,1)S(1)}, u32[]{:S(2)}, u32[]{:S(2)}) collective-permute-start(bf16[512,1152]{1,0:T(8,128)(2,1)S(1)} %copy-done.3), channel_id=1, source_target_pairs={{0,4},{2,6},{4,0},{6,2},{8,12},{10,14},{12,8},{14,10},{16,20},{18,... | collective-permute-start | bytes 3538952 | tf_op jit(solution)/shard_map/ppermute | solution.py:77
  17.3 0.4 collective-permute-start
  17.7 0.8 fusion.80
  18.6 26.7 %collective-permute-done.1 = bf16[256,1152]{1,0:T(8,128)(2,1)S(1)} collective-permute-done((bf16[256,1152]{1,0:T(8,128)(2,1)S(1)}, bf16[256,1152]{1,0:T(8,128)(2,1)S(1)}, u32[]{:S(2)}, u32[]{:S(2)}) %collective-permute-start.1) | collective-permute-done | bytes 589856 | tf_op jit(solution)/shard_map/ppermute | solution.py:77
  45.3 0.2 fusion.69
  45.5 0.7 fusion.64
  46.2 0.6 fusion.65
  46.8 0.3 fusion.68
  47.2 0.6 convolution_add_fusion.1
  47.8 1.0 fusion.48
  48.8 0.9 convolution_convert_fusion
  49.7 1.0 fusion.49
  50.7 0.9 convolution_convert_fusion.1
  51.6 1.0 fusion.50
  52.7 0.9 convolution_convert_fusion.2
  53.6 1.9 %collective-permute-start.8 = (bf16[512,1152]{1,0:T(8,128)(2,1)S(1)}, bf16[512,1152]{1,0:T(8,128)(2,1)S(1)}, u32[]{:S(2)}, u32[]{:S(2)}) collective-permute-start(bf16[512,1152]{1,0:T(8,128)(2,1)S(1)} %convolution_convert_fusion), channel_id=1, source_target_pairs={{0,4},{2,6},{4,0},{6,2},{8,12},{10,14},{12,8},{14,10},{16,20},{18,... | collective-permute-start | bytes 3538952 | tf_op jit(solution)/shard_map/ppermute | solution.py:77
  55.5 1.5 %collective-permute-start.7 = (bf16[512,1152]{1,0:T(8,128)(2,1)S(1)}, bf16[512,1152]{1,0:T(8,128)(2,1)S(1)}, u32[]{:S(2)}, u32[]{:S(2)}) collective-permute-start(bf16[512,1152]{1,0:T(8,128)(2,1)S(1)} %convolution_convert_fusion.1), channel_id=1, source_target_pairs={{0,1},{1,0},{2,3},{3,2},{4,5},{5,4},{6,7},{7,6},{8,9},{9,8},{10,11... | collective-permute-start | bytes 3538952 | tf_op jit(solution)/shard_map/ppermute | solution.py:77
  57.0 0.3 fusion.14
  57.4 0.8 fusion.81
  58.2 0.4 copy-done.1
  58.6 0.3 fusion.13
  58.9 0.8 fusion.82
  59.8 10.8 %collective-permute-done = bf16[256,1152]{1,0:T(8,128)(2,1)S(1)} collective-permute-done((bf16[256,1152]{1,0:T(8,128)(2,1)S(1)}, bf16[256,1152]{1,0:T(8,128)(2,1)S(1)}, u32[]{:S(2)}, u32[]{:S(2)}) %collective-permute-start) | collective-permute-done | bytes 589856 | tf_op jit(solution)/shard_map/ppermute | solution.py:77
  70.8 0.7 fusion.63
  71.4 0.6 fusion.70
  72.1 0.3 fusion.73
  72.5 2.9 %collective-permute-start.12 = (bf16[128,1152]{1,0:T(8,128)(2,1)S(1)}, bf16[128,1152]{1,0:T(8,128)(2,1)S(1)}, u32[]{:S(2)}, u32[]{:S(2)}) collective-permute-start(bf16[128,1152]{1,0:T(8,128)(2,1)S(1)} %slice.22), channel_id=1, source_target_pairs={{0,16},{2,18},{4,20},{6,22},{8,24},{10,26},{12,28},{14,30},{16,0},... | collective-permute-start | bytes 884744 | tf_op jit(solution)/shard_map/ppermute | solution.py:77
  75.4 0.8 fusion.77
  76.2 1.3 %fusion.10 = (f32[512]{0:T(512)S(1)}, f32[512,1152]{1,0:T(8,128)S(1)}) fusion(bf16[512,1152]{1,0:T(8,128)(2,1)S(1)} %copy-done.1, f32[512]{0:T(512)S(1)} %add_rsqrt_fusion.1, f32[512,1152]{1,0:T(8,128)S(1)} %fusion.77, f32[512,1152]{1,0:T(8,128)S(1)} %fusion.82, f32[512,1152]{1,0:T(8,128)S(1)} %fusion.81, f32[512,1152]{1,0:T(8,128)S(1)} %convolution_add_fusion.1, ...), kind=kOutput, calls=%fused_computation.19 | convolution fusion | flops 608697856 | bytes 14684160 | tf_op jit(solution)/shard_map/dot_general | solution.py:132
  77.5 4.6 %collective-permute-done.8 = bf16[512,1152]{1,0:T(8,128)(2,1)S(1)} collective-permute-done((bf16[512,1152]{1,0:T(8,128)(2,1)S(1)}, bf16[512,1152]{1,0:T(8,128)(2,1)S(1)}, u32[]{:S(2)}, u32[]{:S(2)}) %collective-permute-start.8) | collective-permute-done | bytes 1179680 | tf_op jit(solution)/shard_map/ppermute | solution.py:77
  82.1 1.5 %collective-permute-done.7 = bf16[512,1152]{1,0:T(8,128)(2,1)S(1)} collective-permute-done((bf16[512,1152]{1,0:T(8,128)(2,1)S(1)}, bf16[512,1152]{1,0:T(8,128)(2,1)S(1)}, u32[]{:S(2)}, u32[]{:S(2)}) %collective-permute-start.7) | collective-permute-done | bytes 1179680 | tf_op jit(solution)/shard_map/ppermute | solution.py:77
  83.5 1.5 %fusion.7 = (f32[512]{0:T(512)S(1)}, f32[512,1152]{1,0:T(8,128)S(1)}) fusion(bf16[512,1152]{1,0:T(8,128)(2,1)S(1)} %copy-done, f32[512]{0:T(512)S(1)} %add_rsqrt_fusion, bf16[512,1152]{1,0:T(8,128)(2,1)S(1)} %collective-permute-done.8, bf16[512,1152]{1,0:T(8,128)(2,1)S(1)} %collective-permute-done.7, bf16[512,1152]{1,0:T(8,128)(2,1)S(1)} %collective-permute-done.5, ...), kind=kOutput, calls=%fused_computation.16 | convolution fusion | flops 609877504 | bytes 8785920 | tf_op jit(solution)/shard_map/dot_general | solution.py:104
  85.0 0.9 fusion.9.base
  85.9 1.9 %fusion.12 = f32[512,1152]{1,0:T(8,128)} fusion(f32[512,1152]{1,0:T(8,128)S(1)} %get-tuple-element.47, bf16[512,1152]{1,0:T(8,128)(2,1)S(1)} %copy-done.1, f32[512]{0:T(512)S(1)} %get-tuple-element.46, f32[512]{0:T(512)S(1)} %add_rsqrt_fusion.1), kind=kLoop, calls=%fused_computation.21 | loop fusion | flops 2949120 | bytes 5902336 | tf_op jit(solution)/shard_map/mul | solution.py:110
  87.8 6.5 %collective-permute-done.9.refs_0_ = bf16[256,1152]{1,0:T(8,128)(2,1)S(1)} collective-permute-done((bf16[256,1152]{1,0:T(8,128)(2,1)S(1)}, bf16[256,1152]{1,0:T(8,128)(2,1)S(1)}, u32[]{:S(2)}, u32[]{:S(2)}) %collective-permute-start.9) | collective-permute-done | bytes 589856 | tf_op jit(solution)/shard_map/ppermute | solution.py:77
  94.3 1.9 %collective-permute-start.10 = (bf16[32,1152]{1,0:T(8,128)(2,1)S(1)}, bf16[32,1152]{1,0:T(8,128)(2,1)S(1)}, u32[]{:S(2)}, u32[]{:S(2)}) collective-permute-start(bf16[32,1152]{1,0:T(8,128)(2,1)S(1)} %slice.20), channel_id=1, source_target_pairs={{0,16},{2,18},{4,20},{6,22},{16,0},{18,2},{20,4},{22,6},{1,17},{3,... | collective-permute-start | bytes 221192 | tf_op jit(solution)/shard_map/ppermute | solution.py:77
  96.2 1.1 %shard_map.60.refs_1_ = f32[512,1152]{1,0:T(8,128)} custom-call(f32[512,1152]{1,0:T(8,128)S(1)} %fusion.9.base, bf16[256,1152]{1,0:T(8,128)(2,1)S(1)} %collective-permute-done.9.refs_0_), custom_call_target="tpu_custom_call" | custom-call | flops 294912 | bytes 2949120 | tf_op jit(solution)/shard_map/pallas_call | solution.py:58
  97.3 1.7 %collective-permute-done.6.refs_0_ = bf16[96,1152]{1,0:T(8,128)(2,1)S(1)} collective-permute-done((bf16[96,1152]{1,0:T(8,128)(2,1)S(1)}, bf16[96,1152]{1,0:T(8,128)(2,1)S(1)}, u32[]{:S(2)}, u32[]{:S(2)}) %collective-permute-start.6) | collective-permute-done | bytes 221216 | tf_op jit(solution)/shard_map/ppermute | solution.py:77
  99.0 0.7 collective-permute-start.11
  99.7 0.8 shard_map.61.refs_1_
  100.5 4.8 %collective-permute-done.12.refs_0_ = bf16[128,1152]{1,0:T(8,128)(2,1)S(1)} collective-permute-done((bf16[128,1152]{1,0:T(8,128)(2,1)S(1)}, bf16[128,1152]{1,0:T(8,128)(2,1)S(1)}, u32[]{:S(2)}, u32[]{:S(2)}) %collective-permute-start.12) | collective-permute-done | bytes 294944 | tf_op jit(solution)/shard_map/ppermute | solution.py:77
  105.3 0.9 shard_map.62.refs_2_
  106.2 0.7 shard_map.63
  (26 shorter events, 0.6 us)
Async XLA Ops:
  1.7 43.5 %collective-permute-start.1 = (bf16[256,1152]{1,0:T(8,128)(2,1)S(1)}, bf16[256,1152]{1,0:T(8,128)(2,1)S(1)}, u32[]{:S(2)}, u32[]{:S(2)}) collective-permute-start(bf16[256,1152]{1,0:T(8,128)(2,1)S(1)} %slice.15), channel_id=1, source_target_pairs={{0,16},{2,18},{4,20},{6,22},{8,24},{10,26},{12,28},{14,30},{16,0},... | collective-permute-start | bytes 1769480 | tf_op jit(solution)/shard_map/ppermute | solution.py:77
  11.2 2.8 %copy-start.3 = (bf16[512,1152]{1,0:T(8,128)(2,1)S(1)}, bf16[512,1152]{1,0:T(8,128)(2,1)}, u32[]{:S(2)}) copy-start(bf16[512,1152]{1,0:T(8,128)(2,1)} %get-tuple-element.27) | copy-start | bytes 3538948
  11.2 6.0 %copy-start = (bf16[512,1152]{1,0:T(8,128)(2,1)S(1)}, bf16[512,1152]{1,0:T(8,128)(2,1)}, u32[]{:S(2)}) copy-start(bf16[512,1152]{1,0:T(8,128)(2,1)} %refs_1_) | copy-start | bytes 3538948
  14.1 33.7 %collective-permute-start.2 = (bf16[512,1152]{1,0:T(8,128)(2,1)S(1)}, bf16[512,1152]{1,0:T(8,128)(2,1)S(1)}, u32[]{:S(2)}, u32[]{:S(2)}) collective-permute-start(bf16[512,1152]{1,0:T(8,128)(2,1)S(1)} %copy-done.3), channel_id=1, source_target_pairs={{0,2},{2,0},{4,6},{6,4},{8,10},{10,8},{12,14},{14,12},{16,18},{18,... | collective-permute-start | bytes 3538952 | tf_op jit(solution)/shard_map/ppermute | solution.py:77
  14.2 33.6 %collective-permute-start.3 = (bf16[512,1152]{1,0:T(8,128)(2,1)S(1)}, bf16[512,1152]{1,0:T(8,128)(2,1)S(1)}, u32[]{:S(2)}, u32[]{:S(2)}) collective-permute-start(bf16[512,1152]{1,0:T(8,128)(2,1)S(1)} %copy-done.3), channel_id=1, source_target_pairs={{0,1},{1,0},{2,3},{3,2},{4,5},{5,4},{6,7},{7,6},{8,9},{9,8},{10,11... | collective-permute-start | bytes 3538952 | tf_op jit(solution)/shard_map/ppermute | solution.py:77
  15.7 32.0 %collective-permute-start.4 = (bf16[512,1152]{1,0:T(8,128)(2,1)S(1)}, bf16[512,1152]{1,0:T(8,128)(2,1)S(1)}, u32[]{:S(2)}, u32[]{:S(2)}) collective-permute-start(bf16[512,1152]{1,0:T(8,128)(2,1)S(1)} %copy-done.3), channel_id=1, source_target_pairs={{0,4},{2,6},{4,0},{6,2},{8,12},{10,14},{12,8},{14,10},{16,20},{18,... | collective-permute-start | bytes 3538952 | tf_op jit(solution)/shard_map/ppermute | solution.py:77
  17.3 28.2 %copy-start.2 = (bf16[512,1152]{1,0:T(8,128)(2,1)S(1)}, bf16[512,1152]{1,0:T(8,128)(2,1)}, u32[]{:S(2)}) copy-start(bf16[512,1152]{1,0:T(8,128)(2,1)} %get-tuple-element.24) | copy-start | bytes 3538948
  17.3 53.3 %collective-permute-start = (bf16[256,1152]{1,0:T(8,128)(2,1)S(1)}, bf16[256,1152]{1,0:T(8,128)(2,1)S(1)}, u32[]{:S(2)}, u32[]{:S(2)}) collective-permute-start(bf16[256,1152]{1,0:T(8,128)(2,1)S(1)} %slice.16), channel_id=1, source_target_pairs={{0,16},{2,18},{4,20},{6,22},{8,24},{10,26},{12,28},{14,30},{16,0},... | collective-permute-start | bytes 1769480 | tf_op jit(solution)/shard_map/ppermute | solution.py:77
  47.1 47.2 %collective-permute-start.9 = (bf16[256,1152]{1,0:T(8,128)(2,1)S(1)}, bf16[256,1152]{1,0:T(8,128)(2,1)S(1)}, u32[]{:S(2)}, u32[]{:S(2)}) collective-permute-start(bf16[256,1152]{1,0:T(8,128)(2,1)S(1)} %fusion.68), channel_id=1, source_target_pairs={{0,16},{2,18},{4,20},{6,22},{8,24},{10,26},{12,28},{14,30},{16,0},... | collective-permute-start | bytes 1769480 | tf_op jit(solution)/shard_map/ppermute | solution.py:77
  53.5 17.0 %collective-permute-start.5 = (bf16[512,1152]{1,0:T(8,128)(2,1)S(1)}, bf16[512,1152]{1,0:T(8,128)(2,1)S(1)}, u32[]{:S(2)}, u32[]{:S(2)}) collective-permute-start(bf16[512,1152]{1,0:T(8,128)(2,1)S(1)} %convolution_convert_fusion.2), channel_id=1, source_target_pairs={{0,2},{2,0},{4,6},{6,4},{8,10},{10,8},{12,14},{14,12},{16,18},{18,... | collective-permute-start | bytes 3538952 | tf_op jit(solution)/shard_map/ppermute | solution.py:77
  53.6 28.5 %collective-permute-start.8 = (bf16[512,1152]{1,0:T(8,128)(2,1)S(1)}, bf16[512,1152]{1,0:T(8,128)(2,1)S(1)}, u32[]{:S(2)}, u32[]{:S(2)}) collective-permute-start(bf16[512,1152]{1,0:T(8,128)(2,1)S(1)} %convolution_convert_fusion), channel_id=1, source_target_pairs={{0,4},{2,6},{4,0},{6,2},{8,12},{10,14},{12,8},{14,10},{16,20},{18,... | collective-permute-start | bytes 3538952 | tf_op jit(solution)/shard_map/ppermute | solution.py:77
  55.5 28.0 %collective-permute-start.7 = (bf16[512,1152]{1,0:T(8,128)(2,1)S(1)}, bf16[512,1152]{1,0:T(8,128)(2,1)S(1)}, u32[]{:S(2)}, u32[]{:S(2)}) collective-permute-start(bf16[512,1152]{1,0:T(8,128)(2,1)S(1)} %convolution_convert_fusion.1), channel_id=1, source_target_pairs={{0,1},{1,0},{2,3},{3,2},{4,5},{5,4},{6,7},{7,6},{8,9},{9,8},{10,11... | collective-permute-start | bytes 3538952 | tf_op jit(solution)/shard_map/ppermute | solution.py:77
  57.3 1.3 %copy-start.1 = (bf16[512,1152]{1,0:T(8,128)(2,1)S(1)}, bf16[512,1152]{1,0:T(8,128)(2,1)}, u32[]{:S(2)}) copy-start(bf16[512,1152]{1,0:T(8,128)(2,1)} %refs_0_) | copy-start | bytes 3538948
  72.4 26.6 %collective-permute-start.6 = (bf16[96,1152]{1,0:T(8,128)(2,1)S(1)}, bf16[96,1152]{1,0:T(8,128)(2,1)S(1)}, u32[]{:S(2)}, u32[]{:S(2)}) collective-permute-start(bf16[96,1152]{1,0:T(8,128)(2,1)S(1)} %slice.21), channel_id=1, source_target_pairs={{0,16},{2,18},{4,20},{6,22},{8,24},{10,26},{12,28},{14,30},{16,0},... | collective-permute-start | bytes 663560 | tf_op jit(solution)/shard_map/ppermute | solution.py:77
  72.5 32.8 %collective-permute-start.12 = (bf16[128,1152]{1,0:T(8,128)(2,1)S(1)}, bf16[128,1152]{1,0:T(8,128)(2,1)S(1)}, u32[]{:S(2)}, u32[]{:S(2)}) collective-permute-start(bf16[128,1152]{1,0:T(8,128)(2,1)S(1)} %slice.22), channel_id=1, source_target_pairs={{0,16},{2,18},{4,20},{6,22},{8,24},{10,26},{12,28},{14,30},{16,0},... | collective-permute-start | bytes 884744 | tf_op jit(solution)/shard_map/ppermute | solution.py:77
  94.3 11.9 %collective-permute-start.10 = (bf16[32,1152]{1,0:T(8,128)(2,1)S(1)}, bf16[32,1152]{1,0:T(8,128)(2,1)S(1)}, u32[]{:S(2)}, u32[]{:S(2)}) collective-permute-start(bf16[32,1152]{1,0:T(8,128)(2,1)S(1)} %slice.20), channel_id=1, source_target_pairs={{0,16},{2,18},{4,20},{6,22},{16,0},{18,2},{20,4},{22,6},{1,17},{3,... | collective-permute-start | bytes 221192 | tf_op jit(solution)/shard_map/ppermute | solution.py:77
  99.0 7.2 %collective-permute-start.11 = (bf16[32,1152]{1,0:T(8,128)(2,1)S(1)}, bf16[32,1152]{1,0:T(8,128)(2,1)S(1)}, u32[]{:S(2)}, u32[]{:S(2)}) collective-permute-start(bf16[32,1152]{1,0:T(8,128)(2,1)S(1)} %slice.20), channel_id=1, source_target_pairs={{8,24},{10,26},{12,28},{14,30},{24,8},{26,10},{28,12},{30,14},{9,2... | collective-permute-start | bytes 221192 | tf_op jit(solution)/shard_map/ppermute | solution.py:77

commit v2 on v1

--- a/solution.py
+++ b/solution.py
@@ -112,7 +112,8 @@
 
 def per_device(img_emb, txt_emb, logit_scale, logit_bias):
     top_bit = lax.axis_size("dx").bit_length() - 2
-    half = txt_emb.shape[0] // 2
+    half = txt_emb.shape[0] * 7 // 16 // STEP * STEP
+    second = txt_emb.shape[0] - half
 
     def odd(index):
         return index >> (top_bit - 1) & 1
@@ -160,8 +161,8 @@
     raw, _, near_back = lax.optimization_barrier((far_raw[1], near_partials, near_back))
     more, partial_value = far_part(raw)
     grad_i = grad_i + more
-    most = half * 3 // 8 // STEP * STEP
-    last = half - STEP
+    most = second - 5 * STEP
+    last = second - STEP
     far_back.append(from_partner(partial_value[:most], "dx", top_bit))
     far_back.append(from_partner(partial_value[most:last], "dx", top_bit))
     rest = partial_value[last:]

time: 107 us -> 107 us (level)
  no operation moved by 1% of the time
where the time goes in v2:
time: 107 us
  waiting for transfers between devices  56.6 us (53%)
  matrix products  18.1 us (17%)
  starting transfers between devices  16.8 us (16%)
  Pallas kernels  7.54 us (7%)
  other arithmetic  4.36 us (4%)
  between operations  2.39 us (2%)
  local copies, waits for them, and re-layouts  1.21 us (1%)
    ppermute x13, waiting for transfers between devices, from_partner(): return lax.ppermute(value, axis, pairs)  56.6 us
    ppermute x13, starting transfers between devices, from_partner(): return lax.ppermute(value, axis, pairs)  16.8 us
    dot_general x6, matrix products, tile_weights(): lax.dot_general(images, texts, (((1,), (1,)), ((), ())), preferred_elemen...  7.22 us
    dot_general x6, matrix products, transposed(): lax.dot_general(coeffs, images, (((0,), (0,)), ((), ())), preferred_eleme...  5.34 us
    dot_general x5, matrix products, forward_part(): more = jnp.dot(coeffs, far_txt, preferred_element_type=jnp.float32)  4.72 us
    pallas_call x1, Pallas kernels, rounded_units(): pl.pallas_call(unit_kernel, grid=(4,), out_shape=(shape, shape), in_specs...  4.08 us
    pallas_call x4, Pallas kernels, add_rows(): pl.pallas_call(functools.partial(add_kernel, offsets, odd), out_shape=jax...  3.46 us
    mul x2, other arithmetic, finish(): inverse * (grads - unit * jnp.sum(unit * grads, axis=-1, keepdims=True))  2.73 us
  transfers between devices with their start and end apart: 13, of which 7 were waited for; matrix products, arithmetic and copies ran while one was open for 21% of the time, Pallas kernels for 6%

profile of v2, /device:TPU:0, one launch (start us, length us, event | category | flops | bytes accessed | tf_op | source)
XLA Modules:
  0.0 107.0 jit_solution(5137773661908839580)
XLA Ops:
  0.6 1.1 %slice.15 = bf16[224,1152]{1,0:T(8,128)(2,1)S(1)} slice(bf16[512,1152]{1,0:T(8,128)(2,1)} %refs_1_), slice={[0:224], [0:1152]} | slice | bytes 1032192 | tf_op jit(solution)/shard_map/slice | solution.py:121
  1.7 4.1 %collective-permute-start.1 = (bf16[224,1152]{1,0:T(8,128)(2,1)S(1)}, bf16[224,1152]{1,0:T(8,128)(2,1)S(1)}, u32[]{:S(2)}, u32[]{:S(2)}) collective-permute-start(bf16[224,1152]{1,0:T(8,128)(2,1)S(1)} %slice.15), channel_id=1, source_target_pairs={{0,16},{2,18},{4,20},{6,22},{8,24},{10,26},{12,28},{14,30},{16,0},... | collective-permute-start | bytes 1548296 | tf_op jit(solution)/shard_map/ppermute | solution.py:77
  7.1 4.1 %shard_map.59 = (bf16[512,1152]{1,0:T(8,128)(2,1)}, bf16[512,1152]{1,0:T(8,128)(2,1)}) custom-call(bf16[512,1152]{1,0:T(8,128)(2,1)} %refs_0_, bf16[512,1152]{1,0:T(8,128)(2,1)} %refs_1_), custom_call_target="tpu_custom_call" | custom-call | tf_op jit(solution)/shard_map/pallas_call | solution.py:24
  11.2 2.8 %fusion.49 = bf16[512,512]{1,0:T(8,128)(2,1)S(1)} fusion(bf16[512,1152]{1,0:T(8,128)(2,1)} %get-tuple-element.24, bf16[512,1152]{1,0:T(8,128)(2,1)} %get-tuple-element.27, f32[]{:T(128)} %bitcast.41, f32[]{:T(128)} %bitcast.39), kind=kOutput, calls=%fused_computation.65 | convolution fusion | flops 607125504 | bytes 2883592 | tf_op jit(solution)/shard_map/dot_general | solution.py:89
  14.1 1.6 %collective-permute-start.3 = (bf16[512,1152]{1,0:T(8,128)(2,1)S(1)}, bf16[512,1152]{1,0:T(8,128)(2,1)S(1)}, u32[]{:S(2)}, u32[]{:S(2)}) collective-permute-start(bf16[512,1152]{1,0:T(8,128)(2,1)S(1)} %copy-done.3), channel_id=1, source_target_pairs={{0,1},{1,0},{2,3},{3,2},{4,5},{5,4},{6,7},{7,6},{8,9},{9,8},{10,11... | collective-permute-start | bytes 3538952 | tf_op jit(solution)/shard_map/ppermute | solution.py:77
  15.7 1.5 %collective-permute-start.4 = (bf16[512,1152]{1,0:T(8,128)(2,1)S(1)}, bf16[512,1152]{1,0:T(8,128)(2,1)S(1)}, u32[]{:S(2)}, u32[]{:S(2)}) collective-permute-start(bf16[512,1152]{1,0:T(8,128)(2,1)S(1)} %copy-done.3), channel_id=1, source_target_pairs={{0,4},{2,6},{4,0},{6,2},{8,12},{10,14},{12,8},{14,10},{16,20},{18,... | collective-permute-start | bytes 3538952 | tf_op jit(solution)/shard_map/ppermute | solution.py:77
  17.3 0.4 collective-permute-start
  17.7 0.8 fusion.81
  18.5 25.1 %collective-permute-done.1 = bf16[224,1152]{1,0:T(8,128)(2,1)S(1)} collective-permute-done((bf16[224,1152]{1,0:T(8,128)(2,1)S(1)}, bf16[224,1152]{1,0:T(8,128)(2,1)S(1)}, u32[]{:S(2)}, u32[]{:S(2)}) %collective-permute-start.1) | collective-permute-done | bytes 516128 | tf_op jit(solution)/shard_map/ppermute | solution.py:77
  43.7 0.2 fusion.74
  43.9 0.6 fusion.69
  44.5 0.6 fusion.70
  45.1 0.3 fusion.73
  45.4 0.6 convolution_add_fusion.1
  46.1 1.0 fusion.50
  47.1 0.9 convolution_convert_fusion
  48.0 1.0 fusion.51
  49.0 0.9 convolution_convert_fusion.1
  49.9 1.0 fusion.52
  50.9 0.9 convolution_convert_fusion.2
  51.9 1.9 %collective-permute-start.8 = (bf16[512,1152]{1,0:T(8,128)(2,1)S(1)}, bf16[512,1152]{1,0:T(8,128)(2,1)S(1)}, u32[]{:S(2)}, u32[]{:S(2)}) collective-permute-start(bf16[512,1152]{1,0:T(8,128)(2,1)S(1)} %convolution_convert_fusion), channel_id=1, source_target_pairs={{0,4},{2,6},{4,0},{6,2},{8,12},{10,14},{12,8},{14,10},{16,20},{18,... | collective-permute-start | bytes 3538952 | tf_op jit(solution)/shard_map/ppermute | solution.py:77
  53.8 1.5 %collective-permute-start.7 = (bf16[512,1152]{1,0:T(8,128)(2,1)S(1)}, bf16[512,1152]{1,0:T(8,128)(2,1)S(1)}, u32[]{:S(2)}, u32[]{:S(2)}) collective-permute-start(bf16[512,1152]{1,0:T(8,128)(2,1)S(1)} %convolution_convert_fusion.1), channel_id=1, source_target_pairs={{0,1},{1,0},{2,3},{3,2},{4,5},{5,4},{6,7},{7,6},{8,9},{9,8},{10,11... | collective-permute-start | bytes 3538952 | tf_op jit(solution)/shard_map/ppermute | solution.py:77
  55.3 0.3 fusion.14
  55.7 0.3 fusion.13
  56.0 0.8 fusion.82
  56.8 0.8 fusion.83
  57.7 11.3 %collective-permute-done = bf16[288,1152]{1,0:T(8,128)(2,1)S(1)} collective-permute-done((bf16[288,1152]{1,0:T(8,128)(2,1)S(1)}, bf16[288,1152]{1,0:T(8,128)(2,1)S(1)}, u32[]{:S(2)}, u32[]{:S(2)}) %collective-permute-start) | collective-permute-done | bytes 663584 | tf_op jit(solution)/shard_map/ppermute | solution.py:77
  69.0 0.2 fusion.45
  69.2 0.7 fusion.68
  69.9 0.7 fusion.41
  70.5 0.3 fusion.44
  71.0 2.9 %collective-permute-start.12 = (bf16[128,1152]{1,0:T(8,128)(2,1)S(1)}, bf16[128,1152]{1,0:T(8,128)(2,1)S(1)}, u32[]{:S(2)}, u32[]{:S(2)}) collective-permute-start(bf16[128,1152]{1,0:T(8,128)(2,1)S(1)} %get-tuple-element.42), channel_id=1, source_target_pairs={{0,16},{2,18},{4,20},{6,22},{8,24},{10,26},{12,28},{14,30},{16,0},... | collective-permute-start | bytes 884744 | tf_op jit(solution)/shard_map/ppermute | solution.py:77
  73.9 1.1 %fusion.75 = f32[512,1152]{1,0:T(8,128)S(1)} fusion(bf16[512,288]{0,1:T(8,128)(2,1)S(1)} %fusion.68, bf16[288,1152]{1,0:T(8,128)(2,1)S(1)} %collective-permute-done, f32[288]{0:T(512)S(1)} %add_rsqrt_fusion.2), kind=kOutput, calls=%fused_computation.96 | convolution fusion | flops 340733952 | bytes 3318912 | tf_op jit(solution)/shard_map/dot_general | solution.py:133
  75.0 1.3 %fusion.10 = (f32[512]{0:T(512)S(1)}, f32[512,1152]{1,0:T(8,128)S(1)}) fusion(bf16[512,1152]{1,0:T(8,128)(2,1)S(1)} %copy-done.1, f32[512]{0:T(512)S(1)} %add_rsqrt_fusion.1, f32[512,1152]{1,0:T(8,128)S(1)} %fusion.75, f32[512,1152]{1,0:T(8,128)S(1)} %fusion.83, f32[512,1152]{1,0:T(8,128)S(1)} %fusion.82, f32[512,1152]{1,0:T(8,128)S(1)} %convolution_add_fusion.1, ...), kind=kOutput, calls=%fused_computation.19 | convolution fusion | flops 608697856 | bytes 14684160 | tf_op jit(solution)/shard_map/dot_general | solution.py:133
  76.3 4.0 %collective-permute-done.8 = bf16[512,1152]{1,0:T(8,128)(2,1)S(1)} collective-permute-done((bf16[512,1152]{1,0:T(8,128)(2,1)S(1)}, bf16[512,1152]{1,0:T(8,128)(2,1)S(1)}, u32[]{:S(2)}, u32[]{:S(2)}) %collective-permute-start.8) | collective-permute-done | bytes 1179680 | tf_op jit(solution)/shard_map/ppermute | solution.py:77
  80.4 1.5 %collective-permute-done.7 = bf16[512,1152]{1,0:T(8,128)(2,1)S(1)} collective-permute-done((bf16[512,1152]{1,0:T(8,128)(2,1)S(1)}, bf16[512,1152]{1,0:T(8,128)(2,1)S(1)}, u32[]{:S(2)}, u32[]{:S(2)}) %collective-permute-start.7) | collective-permute-done | bytes 1179680 | tf_op jit(solution)/shard_map/ppermute | solution.py:77
  81.9 1.5 %fusion.7 = (f32[512]{0:T(512)S(1)}, f32[512,1152]{1,0:T(8,128)S(1)}) fusion(bf16[512,1152]{1,0:T(8,128)(2,1)S(1)} %copy-done, f32[512]{0:T(512)S(1)} %add_rsqrt_fusion, bf16[512,1152]{1,0:T(8,128)(2,1)S(1)} %collective-permute-done.8, bf16[512,1152]{1,0:T(8,128)(2,1)S(1)} %collective-permute-done.7, bf16[512,1152]{1,0:T(8,128)(2,1)S(1)} %collective-permute-done.5, ...), kind=kOutput, calls=%fused_computation.16 | convolution fusion | flops 609877504 | bytes 8785920 | tf_op jit(solution)/shard_map/dot_general | solution.py:104
  83.4 0.9 fusion.9.base
  84.2 1.9 %fusion.12 = f32[512,1152]{1,0:T(8,128)} fusion(f32[512,1152]{1,0:T(8,128)S(1)} %get-tuple-element.49, bf16[512,1152]{1,0:T(8,128)(2,1)S(1)} %copy-done.1, f32[512]{0:T(512)S(1)} %get-tuple-element.48, f32[512]{0:T(512)S(1)} %add_rsqrt_fusion.1), kind=kLoop, calls=%fused_computation.21 | loop fusion | flops 2949120 | bytes 5902336 | tf_op jit(solution)/shard_map/mul | solution.py:110
  86.1 6.6 %collective-permute-done.9.refs_0_ = bf16[224,1152]{1,0:T(8,128)(2,1)S(1)} collective-permute-done((bf16[224,1152]{1,0:T(8,128)(2,1)S(1)}, bf16[224,1152]{1,0:T(8,128)(2,1)S(1)}, u32[]{:S(2)}, u32[]{:S(2)}) %collective-permute-start.9) | collective-permute-done | bytes 516128 | tf_op jit(solution)/shard_map/ppermute | solution.py:77
  92.7 1.9 %collective-permute-start.10 = (bf16[32,1152]{1,0:T(8,128)(2,1)S(1)}, bf16[32,1152]{1,0:T(8,128)(2,1)S(1)}, u32[]{:S(2)}, u32[]{:S(2)}) collective-permute-start(bf16[32,1152]{1,0:T(8,128)(2,1)S(1)} %slice.20), channel_id=1, source_target_pairs={{0,16},{2,18},{4,20},{6,22},{16,0},{18,2},{20,4},{22,6},{1,17},{3,... | collective-permute-start | bytes 221192 | tf_op jit(solution)/shard_map/ppermute | solution.py:77
  94.6 1.0 shard_map.60.refs_1_
  95.6 3.4 %collective-permute-done.6.refs_0_ = bf16[128,1152]{1,0:T(8,128)(2,1)S(1)} collective-permute-done((bf16[128,1152]{1,0:T(8,128)(2,1)S(1)}, bf16[128,1152]{1,0:T(8,128)(2,1)S(1)}, u32[]{:S(2)}, u32[]{:S(2)}) %collective-permute-start.6) | collective-permute-done | bytes 294944 | tf_op jit(solution)/shard_map/ppermute | solution.py:77
  99.0 0.7 collective-permute-start.11
  99.6 0.9 shard_map.61.refs_1_
  100.5 4.7 %collective-permute-done.12.refs_0_ = bf16[128,1152]{1,0:T(8,128)(2,1)S(1)} collective-permute-done((bf16[128,1152]{1,0:T(8,128)(2,1)S(1)}, bf16[128,1152]{1,0:T(8,128)(2,1)S(1)}, u32[]{:S(2)}, u32[]{:S(2)}) %collective-permute-start.12) | collective-permute-done | bytes 294944 | tf_op jit(solution)/shard_map/ppermute | solution.py:77
  105.3 0.9 shard_map.62.refs_2_
  106.1 0.7 shard_map.63
  (25 shorter events, 0.4 us)
Async XLA Ops:
  1.7 42.0 %collective-permute-start.1 = (bf16[224,1152]{1,0:T(8,128)(2,1)S(1)}, bf16[224,1152]{1,0:T(8,128)(2,1)S(1)}, u32[]{:S(2)}, u32[]{:S(2)}) collective-permute-start(bf16[224,1152]{1,0:T(8,128)(2,1)S(1)} %slice.15), channel_id=1, source_target_pairs={{0,16},{2,18},{4,20},{6,22},{8,24},{10,26},{12,28},{14,30},{16,0},... | collective-permute-start | bytes 1548296 | tf_op jit(solution)/shard_map/ppermute | solution.py:77
  11.2 2.8 %copy-start.3 = (bf16[512,1152]{1,0:T(8,128)(2,1)S(1)}, bf16[512,1152]{1,0:T(8,128)(2,1)}, u32[]{:S(2)}) copy-start(bf16[512,1152]{1,0:T(8,128)(2,1)} %get-tuple-element.27) | copy-start | bytes 3538948
  11.2 6.0 %copy-start = (bf16[512,1152]{1,0:T(8,128)(2,1)S(1)}, bf16[512,1152]{1,0:T(8,128)(2,1)}, u32[]{:S(2)}) copy-start(bf16[512,1152]{1,0:T(8,128)(2,1)} %refs_1_) | copy-start | bytes 3538948
  14.1 32.0 %collective-permute-start.2 = (bf16[512,1152]{1,0:T(8,128)(2,1)S(1)}, bf16[512,1152]{1,0:T(8,128)(2,1)S(1)}, u32[]{:S(2)}, u32[]{:S(2)}) collective-permute-start(bf16[512,1152]{1,0:T(8,128)(2,1)S(1)} %copy-done.3), channel_id=1, source_target_pairs={{0,2},{2,0},{4,6},{6,4},{8,10},{10,8},{12,14},{14,12},{16,18},{18,... | collective-permute-start | bytes 3538952 | tf_op jit(solution)/shard_map/ppermute | solution.py:77
  14.1 32.0 %collective-permute-start.3 = (bf16[512,1152]{1,0:T(8,128)(2,1)S(1)}, bf16[512,1152]{1,0:T(8,128)(2,1)S(1)}, u32[]{:S(2)}, u32[]{:S(2)}) collective-permute-start(bf16[512,1152]{1,0:T(8,128)(2,1)S(1)} %copy-done.3), channel_id=1, source_target_pairs={{0,1},{1,0},{2,3},{3,2},{4,5},{5,4},{6,7},{7,6},{8,9},{9,8},{10,11... | collective-permute-start | bytes 3538952 | tf_op jit(solution)/shard_map/ppermute | solution.py:77
  15.7 30.4 %collective-permute-start.4 = (bf16[512,1152]{1,0:T(8,128)(2,1)S(1)}, bf16[512,1152]{1,0:T(8,128)(2,1)S(1)}, u32[]{:S(2)}, u32[]{:S(2)}) collective-permute-start(bf16[512,1152]{1,0:T(8,128)(2,1)S(1)} %copy-done.3), channel_id=1, source_target_pairs={{0,4},{2,6},{4,0},{6,2},{8,12},{10,14},{12,8},{14,10},{16,20},{18,... | collective-permute-start | bytes 3538952 | tf_op jit(solution)/shard_map/ppermute | solution.py:77
  17.3 26.6 %copy-start.2 = (bf16[512,1152]{1,0:T(8,128)(2,1)S(1)}, bf16[512,1152]{1,0:T(8,128)(2,1)}, u32[]{:S(2)}) copy-start(bf16[512,1152]{1,0:T(8,128)(2,1)} %get-tuple-element.24) | copy-start | bytes 3538948
  17.3 51.7 %collective-permute-start = (bf16[288,1152]{1,0:T(8,128)(2,1)S(1)}, bf16[288,1152]{1,0:T(8,128)(2,1)S(1)}, u32[]{:S(2)}, u32[]{:S(2)}) collective-permute-start(bf16[288,1152]{1,0:T(8,128)(2,1)S(1)} %slice.16), channel_id=1, source_target_pairs={{0,16},{2,18},{4,20},{6,22},{8,24},{10,26},{12,28},{14,30},{16,0},... | collective-permute-start | bytes 1990664 | tf_op jit(solution)/shard_map/ppermute | solution.py:77
  45.4 47.3 %collective-permute-start.9 = (bf16[224,1152]{1,0:T(8,128)(2,1)S(1)}, bf16[224,1152]{1,0:T(8,128)(2,1)S(1)}, u32[]{:S(2)}, u32[]{:S(2)}) collective-permute-start(bf16[224,1152]{1,0:T(8,128)(2,1)S(1)} %fusion.73), channel_id=1, source_target_pairs={{0,16},{2,18},{4,20},{6,22},{8,24},{10,26},{12,28},{14,30},{16,0},... | collective-permute-start | bytes 1548296 | tf_op jit(solution)/shard_map/ppermute | solution.py:77
  51.8 3.8 %copy-start.1 = (bf16[512,1152]{1,0:T(8,128)(2,1)S(1)}, bf16[512,1152]{1,0:T(8,128)(2,1)}, u32[]{:S(2)}) copy-start(bf16[512,1152]{1,0:T(8,128)(2,1)} %refs_0_) | copy-start | bytes 3538948
  51.8 17.1 %collective-permute-start.5 = (bf16[512,1152]{1,0:T(8,128)(2,1)S(1)}, bf16[512,1152]{1,0:T(8,128)(2,1)S(1)}, u32[]{:S(2)}, u32[]{:S(2)}) collective-permute-start(bf16[512,1152]{1,0:T(8,128)(2,1)S(1)} %convolution_convert_fusion.2), channel_id=1, source_target_pairs={{0,2},{2,0},{4,6},{6,4},{8,10},{10,8},{12,14},{14,12},{16,18},{18,... | collective-permute-start | bytes 3538952 | tf_op jit(solution)/shard_map/ppermute | solution.py:77
  51.9 28.5 %collective-permute-start.8 = (bf16[512,1152]{1,0:T(8,128)(2,1)S(1)}, bf16[512,1152]{1,0:T(8,128)(2,1)S(1)}, u32[]{:S(2)}, u32[]{:S(2)}) collective-permute-start(bf16[512,1152]{1,0:T(8,128)(2,1)S(1)} %convolution_convert_fusion), channel_id=1, source_target_pairs={{0,4},{2,6},{4,0},{6,2},{8,12},{10,14},{12,8},{14,10},{16,20},{18,... | collective-permute-start | bytes 3538952 | tf_op jit(solution)/shard_map/ppermute | solution.py:77
  53.8 28.0 %collective-permute-start.7 = (bf16[512,1152]{1,0:T(8,128)(2,1)S(1)}, bf16[512,1152]{1,0:T(8,128)(2,1)S(1)}, u32[]{:S(2)}, u32[]{:S(2)}) collective-permute-start(bf16[512,1152]{1,0:T(8,128)(2,1)S(1)} %convolution_convert_fusion.1), channel_id=1, source_target_pairs={{0,1},{1,0},{2,3},{3,2},{4,5},{5,4},{6,7},{7,6},{8,9},{9,8},{10,11... | collective-permute-start | bytes 3538952 | tf_op jit(solution)/shard_map/ppermute | solution.py:77
  70.9 28.0 %collective-permute-start.6 = (bf16[128,1152]{1,0:T(8,128)(2,1)S(1)}, bf16[128,1152]{1,0:T(8,128)(2,1)S(1)}, u32[]{:S(2)}, u32[]{:S(2)}) collective-permute-start(bf16[128,1152]{1,0:T(8,128)(2,1)S(1)} %get-tuple-element.43), channel_id=1, source_target_pairs={{0,16},{2,18},{4,20},{6,22},{8,24},{10,26},{12,28},{14,30},{16,0},... | collective-permute-start | bytes 884744 | tf_op jit(solution)/shard_map/ppermute | solution.py:77
  71.0 34.2 %collective-permute-start.12 = (bf16[128,1152]{1,0:T(8,128)(2,1)S(1)}, bf16[128,1152]{1,0:T(8,128)(2,1)S(1)}, u32[]{:S(2)}, u32[]{:S(2)}) collective-permute-start(bf16[128,1152]{1,0:T(8,128)(2,1)S(1)} %get-tuple-element.42), channel_id=1, source_target_pairs={{0,16},{2,18},{4,20},{6,22},{8,24},{10,26},{12,28},{14,30},{16,0},... | collective-permute-start | bytes 884744 | tf_op jit(solution)/shard_map/ppermute | solution.py:77
  92.7 13.5 %collective-permute-start.10 = (bf16[32,1152]{1,0:T(8,128)(2,1)S(1)}, bf16[32,1152]{1,0:T(8,128)(2,1)S(1)}, u32[]{:S(2)}, u32[]{:S(2)}) collective-permute-start(bf16[32,1152]{1,0:T(8,128)(2,1)S(1)} %slice.20), channel_id=1, source_target_pairs={{0,16},{2,18},{4,20},{6,22},{16,0},{18,2},{20,4},{22,6},{1,17},{3,... | collective-permute-start | bytes 221192 | tf_op jit(solution)/shard_map/ppermute | solution.py:77
  99.0 7.2 %collective-permute-start.11 = (bf16[32,1152]{1,0:T(8,128)(2,1)S(1)}, bf16[32,1152]{1,0:T(8,128)(2,1)S(1)}, u32[]{:S(2)}, u32[]{:S(2)}) collective-permute-start(bf16[32,1152]{1,0:T(8,128)(2,1)S(1)} %slice.20), channel_id=1, source_target_pairs={{8,24},{10,26},{12,28},{14,30},{24,8},{26,10},{28,12},{30,14},{9,2... | collective-permute-start | bytes 221192 | tf_op jit(solution)/shard_map/ppermute | solution.py:77

commit v3 on v2

--- a/solution.py
+++ b/solution.py
@@ -181,7 +181,8 @@
     odd_back = from_partner(rest, "dx", top_bit, odd)
     grad_txt = add_rows(base, [far_back[1]], (half,), grad_txt)
     grad_txt = add_rows(base, [far_back[2]], (half + most,), grad_txt)
-    grad_txt = add_rows(base, [even_back, odd_back], (half + last,), grad_txt, odd)
+    end = base[half + last :] + (even_back.astype(jnp.float32) + odd_back.astype(jnp.float32))
+    grad_txt = lax.dynamic_update_slice(grad_txt, end, (half + last, 0))
     return (grad_img, grad_txt)
 
 

time: 107 us -> 107 us (level)
    pallas_call x4 -> x3, Pallas kernels: 3.46 us -> 2.76 us  [add_rows(): pl.pallas_call(functools.partial(add_kernel, offsets, odd), out_shape=jax...]
where the time goes in v3:
time: 107 us
  waiting for transfers between devices  56.6 us (53%)
  matrix products  18.1 us (17%)
  starting transfers between devices  16.8 us (16%)
  Pallas kernels  6.84 us (6%)
  other arithmetic  5.05 us (5%)
  between operations  2.23 us (2%)
  local copies, waits for them, and re-layouts  1.21 us (1%)
    ppermute x13, waiting for transfers between devices, from_partner(): return lax.ppermute(value, axis, pairs)  56.6 us
    ppermute x13, starting transfers between devices, from_partner(): return lax.ppermute(value, axis, pairs)  16.8 us
    dot_general x6, matrix products, tile_weights(): lax.dot_general(images, texts, (((1,), (1,)), ((), ())), preferred_elemen...  7.22 us
    dot_general x6, matrix products, transposed(): lax.dot_general(coeffs, images, (((0,), (0,)), ((), ())), preferred_eleme...  5.34 us
    dot_general x5, matrix products, forward_part(): more = jnp.dot(coeffs, far_txt, preferred_element_type=jnp.float32)  4.72 us
    pallas_call x1, Pallas kernels, rounded_units(): pl.pallas_call(unit_kernel, grid=(4,), out_shape=(shape, shape), in_specs...  4.08 us
    pallas_call x3, Pallas kernels, add_rows(): pl.pallas_call(functools.partial(add_kernel, offsets, odd), out_shape=jax...  2.76 us
    mul x2, other arithmetic, finish(): inverse * (grads - unit * jnp.sum(unit * grads, axis=-1, keepdims=True))  2.73 us
  transfers between devices with their start and end apart: 13, of which 7 were waited for; matrix products, arithmetic and copies ran while one was open for 21% of the time, Pallas kernels for 6%

profile of v3, /device:TPU:0, one launch (start us, length us, event | category | flops | bytes accessed | tf_op | source)
XLA Modules:
  0.0 106.8 jit_solution(7947844023657639814)
XLA Ops:
  0.6 1.1 %slice.18 = bf16[224,1152]{1,0:T(8,128)(2,1)S(1)} slice(bf16[512,1152]{1,0:T(8,128)(2,1)} %refs_1_), slice={[0:224], [0:1152]} | slice | bytes 1032192 | tf_op jit(solution)/shard_map/slice | solution.py:121
  1.7 4.1 %collective-permute-start.1 = (bf16[224,1152]{1,0:T(8,128)(2,1)S(1)}, bf16[224,1152]{1,0:T(8,128)(2,1)S(1)}, u32[]{:S(2)}, u32[]{:S(2)}) collective-permute-start(bf16[224,1152]{1,0:T(8,128)(2,1)S(1)} %slice.18), channel_id=1, source_target_pairs={{0,16},{2,18},{4,20},{6,22},{8,24},{10,26},{12,28},{14,30},{16,0},... | collective-permute-start | bytes 1548296 | tf_op jit(solution)/shard_map/ppermute | solution.py:77
  7.1 4.1 %shard_map.59 = (bf16[512,1152]{1,0:T(8,128)(2,1)}, bf16[512,1152]{1,0:T(8,128)(2,1)}) custom-call(bf16[512,1152]{1,0:T(8,128)(2,1)} %refs_0_, bf16[512,1152]{1,0:T(8,128)(2,1)} %refs_1_), custom_call_target="tpu_custom_call" | custom-call | tf_op jit(solution)/shard_map/pallas_call | solution.py:24
  11.2 2.8 %fusion.49 = bf16[512,512]{1,0:T(8,128)(2,1)S(1)} fusion(bf16[512,1152]{1,0:T(8,128)(2,1)} %get-tuple-element.24, bf16[512,1152]{1,0:T(8,128)(2,1)} %get-tuple-element.27, f32[]{:T(128)} %bitcast.41, f32[]{:T(128)} %bitcast.39), kind=kOutput, calls=%fused_computation.65 | convolution fusion | flops 607125504 | bytes 2883592 | tf_op jit(solution)/shard_map/dot_general | solution.py:89
  14.1 1.6 %collective-permute-start.3 = (bf16[512,1152]{1,0:T(8,128)(2,1)S(1)}, bf16[512,1152]{1,0:T(8,128)(2,1)S(1)}, u32[]{:S(2)}, u32[]{:S(2)}) collective-permute-start(bf16[512,1152]{1,0:T(8,128)(2,1)S(1)} %copy-done.3), channel_id=1, source_target_pairs={{0,1},{1,0},{2,3},{3,2},{4,5},{5,4},{6,7},{7,6},{8,9},{9,8},{10,11... | collective-permute-start | bytes 3538952 | tf_op jit(solution)/shard_map/ppermute | solution.py:77
  15.7 1.5 %collective-permute-start.4 = (bf16[512,1152]{1,0:T(8,128)(2,1)S(1)}, bf16[512,1152]{1,0:T(8,128)(2,1)S(1)}, u32[]{:S(2)}, u32[]{:S(2)}) collective-permute-start(bf16[512,1152]{1,0:T(8,128)(2,1)S(1)} %copy-done.3), channel_id=1, source_target_pairs={{0,4},{2,6},{4,0},{6,2},{8,12},{10,14},{12,8},{14,10},{16,20},{18,... | collective-permute-start | bytes 3538952 | tf_op jit(solution)/shard_map/ppermute | solution.py:77
  17.3 0.4 collective-permute-start
  17.7 0.8 fusion.81
  18.5 25.1 %collective-permute-done.1 = bf16[224,1152]{1,0:T(8,128)(2,1)S(1)} collective-permute-done((bf16[224,1152]{1,0:T(8,128)(2,1)S(1)}, bf16[224,1152]{1,0:T(8,128)(2,1)S(1)}, u32[]{:S(2)}, u32[]{:S(2)}) %collective-permute-start.1) | collective-permute-done | bytes 516128 | tf_op jit(solution)/shard_map/ppermute | solution.py:77
  43.7 0.2 fusion.74
  43.9 0.6 fusion.69
  44.5 0.6 fusion.70
  45.1 0.3 fusion.73
  45.4 0.6 convolution_add_fusion.1
  46.1 1.0 fusion.50
  47.1 0.9 convolution_convert_fusion
  48.0 1.0 fusion.51
  49.0 0.9 convolution_convert_fusion.1
  49.9 1.0 fusion.52
  50.9 0.9 convolution_convert_fusion.2
  51.9 1.9 %collective-permute-start.8 = (bf16[512,1152]{1,0:T(8,128)(2,1)S(1)}, bf16[512,1152]{1,0:T(8,128)(2,1)S(1)}, u32[]{:S(2)}, u32[]{:S(2)}) collective-permute-start(bf16[512,1152]{1,0:T(8,128)(2,1)S(1)} %convolution_convert_fusion), channel_id=1, source_target_pairs={{0,4},{2,6},{4,0},{6,2},{8,12},{10,14},{12,8},{14,10},{16,20},{18,... | collective-permute-start | bytes 3538952 | tf_op jit(solution)/shard_map/ppermute | solution.py:77
  53.8 1.5 %collective-permute-start.7 = (bf16[512,1152]{1,0:T(8,128)(2,1)S(1)}, bf16[512,1152]{1,0:T(8,128)(2,1)S(1)}, u32[]{:S(2)}, u32[]{:S(2)}) collective-permute-start(bf16[512,1152]{1,0:T(8,128)(2,1)S(1)} %convolution_convert_fusion.1), channel_id=1, source_target_pairs={{0,1},{1,0},{2,3},{3,2},{4,5},{5,4},{6,7},{7,6},{8,9},{9,8},{10,11... | collective-permute-start | bytes 3538952 | tf_op jit(solution)/shard_map/ppermute | solution.py:77
  55.3 0.3 fusion.14
  55.7 0.3 fusion.13
  56.0 0.8 fusion.82
  56.8 0.8 fusion.83
  57.7 11.3 %collective-permute-done = bf16[288,1152]{1,0:T(8,128)(2,1)S(1)} collective-permute-done((bf16[288,1152]{1,0:T(8,128)(2,1)S(1)}, bf16[288,1152]{1,0:T(8,128)(2,1)S(1)}, u32[]{:S(2)}, u32[]{:S(2)}) %collective-permute-start) | collective-permute-done | bytes 663584 | tf_op jit(solution)/shard_map/ppermute | solution.py:77
  69.0 0.2 fusion.45
  69.2 0.7 fusion.68
  69.9 0.7 fusion.41
  70.5 0.3 fusion.44
  71.0 2.9 %collective-permute-start.10 = (bf16[128,1152]{1,0:T(8,128)(2,1)S(1)}, bf16[128,1152]{1,0:T(8,128)(2,1)S(1)}, u32[]{:S(2)}, u32[]{:S(2)}) collective-permute-start(bf16[128,1152]{1,0:T(8,128)(2,1)S(1)} %get-tuple-element.42), channel_id=1, source_target_pairs={{0,16},{2,18},{4,20},{6,22},{8,24},{10,26},{12,28},{14,30},{16,0},... | collective-permute-start | bytes 884744 | tf_op jit(solution)/shard_map/ppermute | solution.py:77
  73.9 1.1 %fusion.75 = f32[512,1152]{1,0:T(8,128)S(1)} fusion(bf16[512,288]{0,1:T(8,128)(2,1)S(1)} %fusion.68, bf16[288,1152]{1,0:T(8,128)(2,1)S(1)} %collective-permute-done, f32[288]{0:T(512)S(1)} %add_rsqrt_fusion.2), kind=kOutput, calls=%fused_computation.96 | convolution fusion | flops 340733952 | bytes 3318912 | tf_op jit(solution)/shard_map/dot_general | solution.py:133
  75.0 1.3 %fusion.10 = (f32[512]{0:T(512)S(1)}, f32[512,1152]{1,0:T(8,128)S(1)}) fusion(bf16[512,1152]{1,0:T(8,128)(2,1)S(1)} %copy-done.1, f32[512]{0:T(512)S(1)} %add_rsqrt_fusion.1, f32[512,1152]{1,0:T(8,128)S(1)} %fusion.75, f32[512,1152]{1,0:T(8,128)S(1)} %fusion.83, f32[512,1152]{1,0:T(8,128)S(1)} %fusion.82, f32[512,1152]{1,0:T(8,128)S(1)} %convolution_add_fusion.1, ...), kind=kOutput, calls=%fused_computation.19 | convolution fusion | flops 608697856 | bytes 14684160 | tf_op jit(solution)/shard_map/dot_general | solution.py:133
  76.3 4.0 %collective-permute-done.8 = bf16[512,1152]{1,0:T(8,128)(2,1)S(1)} collective-permute-done((bf16[512,1152]{1,0:T(8,128)(2,1)S(1)}, bf16[512,1152]{1,0:T(8,128)(2,1)S(1)}, u32[]{:S(2)}, u32[]{:S(2)}) %collective-permute-start.8) | collective-permute-done | bytes 1179680 | tf_op jit(solution)/shard_map/ppermute | solution.py:77
  80.4 1.5 %collective-permute-done.7 = bf16[512,1152]{1,0:T(8,128)(2,1)S(1)} collective-permute-done((bf16[512,1152]{1,0:T(8,128)(2,1)S(1)}, bf16[512,1152]{1,0:T(8,128)(2,1)S(1)}, u32[]{:S(2)}, u32[]{:S(2)}) %collective-permute-start.7) | collective-permute-done | bytes 1179680 | tf_op jit(solution)/shard_map/ppermute | solution.py:77
  81.9 1.5 %fusion.7 = (f32[512]{0:T(512)S(1)}, f32[512,1152]{1,0:T(8,128)S(1)}) fusion(bf16[512,1152]{1,0:T(8,128)(2,1)S(1)} %copy-done, f32[512]{0:T(512)S(1)} %add_rsqrt_fusion, bf16[512,1152]{1,0:T(8,128)(2,1)S(1)} %collective-permute-done.8, bf16[512,1152]{1,0:T(8,128)(2,1)S(1)} %collective-permute-done.7, bf16[512,1152]{1,0:T(8,128)(2,1)S(1)} %collective-permute-done.5, ...), kind=kOutput, calls=%fused_computation.16 | convolution fusion | flops 609877504 | bytes 8785920 | tf_op jit(solution)/shard_map/dot_general | solution.py:104
  83.4 0.9 fusion.9.base
  84.2 1.9 %fusion.12 = f32[512,1152]{1,0:T(8,128)} fusion(f32[512,1152]{1,0:T(8,128)S(1)} %get-tuple-element.49, bf16[512,1152]{1,0:T(8,128)(2,1)S(1)} %copy-done.1, f32[512]{0:T(512)S(1)} %get-tuple-element.48, f32[512]{0:T(512)S(1)} %add_rsqrt_fusion.1), kind=kLoop, calls=%fused_computation.21 | loop fusion | flops 2949120 | bytes 5902336 | tf_op jit(solution)/shard_map/mul | solution.py:110
  86.1 6.6 %collective-permute-done.9.refs_0_ = bf16[224,1152]{1,0:T(8,128)(2,1)S(1)} collective-permute-done((bf16[224,1152]{1,0:T(8,128)(2,1)S(1)}, bf16[224,1152]{1,0:T(8,128)(2,1)S(1)}, u32[]{:S(2)}, u32[]{:S(2)}) %collective-permute-start.9) | collective-permute-done | bytes 516128 | tf_op jit(solution)/shard_map/ppermute | solution.py:77
  92.7 1.9 %collective-permute-start.11 = (bf16[32,1152]{1,0:T(8,128)(2,1)S(1)}, bf16[32,1152]{1,0:T(8,128)(2,1)S(1)}, u32[]{:S(2)}, u32[]{:S(2)}) collective-permute-start(bf16[32,1152]{1,0:T(8,128)(2,1)S(1)} %slice.24), channel_id=1, source_target_pairs={{0,16},{2,18},{4,20},{6,22},{16,0},{18,2},{20,4},{22,6},{1,17},{3,... | collective-permute-start | bytes 221192 | tf_op jit(solution)/shard_map/ppermute | solution.py:77
  94.6 1.0 shard_map.60.refs_1_
  95.6 3.4 %collective-permute-done.6.refs_0_ = bf16[128,1152]{1,0:T(8,128)(2,1)S(1)} collective-permute-done((bf16[128,1152]{1,0:T(8,128)(2,1)S(1)}, bf16[128,1152]{1,0:T(8,128)(2,1)S(1)}, u32[]{:S(2)}, u32[]{:S(2)}) %collective-permute-start.6) | collective-permute-done | bytes 294944 | tf_op jit(solution)/shard_map/ppermute | solution.py:77
  99.0 0.7 collective-permute-start.12
  99.6 0.9 shard_map.61.refs_1_
  100.5 4.7 %collective-permute-done.10.refs_0_ = bf16[128,1152]{1,0:T(8,128)(2,1)S(1)} collective-permute-done((bf16[128,1152]{1,0:T(8,128)(2,1)S(1)}, bf16[128,1152]{1,0:T(8,128)(2,1)S(1)}, u32[]{:S(2)}, u32[]{:S(2)}) %collective-permute-start.10) | collective-permute-done | bytes 294944 | tf_op jit(solution)/shard_map/ppermute | solution.py:77
  105.3 0.9 shard_map.62
  106.1 0.7 add_dynamic-update-slice_fusion
  (25 shorter events, 0.4 us)
Async XLA Ops:
  1.7 42.0 %collective-permute-start.1 = (bf16[224,1152]{1,0:T(8,128)(2,1)S(1)}, bf16[224,1152]{1,0:T(8,128)(2,1)S(1)}, u32[]{:S(2)}, u32[]{:S(2)}) collective-permute-start(bf16[224,1152]{1,0:T(8,128)(2,1)S(1)} %slice.18), channel_id=1, source_target_pairs={{0,16},{2,18},{4,20},{6,22},{8,24},{10,26},{12,28},{14,30},{16,0},... | collective-permute-start | bytes 1548296 | tf_op jit(solution)/shard_map/ppermute | solution.py:77
  11.2 2.8 %copy-start.3 = (bf16[512,1152]{1,0:T(8,128)(2,1)S(1)}, bf16[512,1152]{1,0:T(8,128)(2,1)}, u32[]{:S(2)}) copy-start(bf16[512,1152]{1,0:T(8,128)(2,1)} %get-tuple-element.27) | copy-start | bytes 3538948
  11.2 6.0 %copy-start = (bf16[512,1152]{1,0:T(8,128)(2,1)S(1)}, bf16[512,1152]{1,0:T(8,128)(2,1)}, u32[]{:S(2)}) copy-start(bf16[512,1152]{1,0:T(8,128)(2,1)} %refs_1_) | copy-start | bytes 3538948
  14.1 32.0 %collective-permute-start.2 = (bf16[512,1152]{1,0:T(8,128)(2,1)S(1)}, bf16[512,1152]{1,0:T(8,128)(2,1)S(1)}, u32[]{:S(2)}, u32[]{:S(2)}) collective-permute-start(bf16[512,1152]{1,0:T(8,128)(2,1)S(1)} %copy-done.3), channel_id=1, source_target_pairs={{0,2},{2,0},{4,6},{6,4},{8,10},{10,8},{12,14},{14,12},{16,18},{18,... | collective-permute-start | bytes 3538952 | tf_op jit(solution)/shard_map/ppermute | solution.py:77
  14.1 32.0 %collective-permute-start.3 = (bf16[512,1152]{1,0:T(8,128)(2,1)S(1)}, bf16[512,1152]{1,0:T(8,128)(2,1)S(1)}, u32[]{:S(2)}, u32[]{:S(2)}) collective-permute-start(bf16[512,1152]{1,0:T(8,128)(2,1)S(1)} %copy-done.3), channel_id=1, source_target_pairs={{0,1},{1,0},{2,3},{3,2},{4,5},{5,4},{6,7},{7,6},{8,9},{9,8},{10,11... | collective-permute-start | bytes 3538952 | tf_op jit(solution)/shard_map/ppermute | solution.py:77
  15.7 30.4 %collective-permute-start.4 = (bf16[512,1152]{1,0:T(8,128)(2,1)S(1)}, bf16[512,1152]{1,0:T(8,128)(2,1)S(1)}, u32[]{:S(2)}, u32[]{:S(2)}) collective-permute-start(bf16[512,1152]{1,0:T(8,128)(2,1)S(1)} %copy-done.3), channel_id=1, source_target_pairs={{0,4},{2,6},{4,0},{6,2},{8,12},{10,14},{12,8},{14,10},{16,20},{18,... | collective-permute-start | bytes 3538952 | tf_op jit(solution)/shard_map/ppermute | solution.py:77
  17.3 26.6 %copy-start.2 = (bf16[512,1152]{1,0:T(8,128)(2,1)S(1)}, bf16[512,1152]{1,0:T(8,128)(2,1)}, u32[]{:S(2)}) copy-start(bf16[512,1152]{1,0:T(8,128)(2,1)} %get-tuple-element.24) | copy-start | bytes 3538948
  17.3 51.7 %collective-permute-start = (bf16[288,1152]{1,0:T(8,128)(2,1)S(1)}, bf16[288,1152]{1,0:T(8,128)(2,1)S(1)}, u32[]{:S(2)}, u32[]{:S(2)}) collective-permute-start(bf16[288,1152]{1,0:T(8,128)(2,1)S(1)} %slice.19), channel_id=1, source_target_pairs={{0,16},{2,18},{4,20},{6,22},{8,24},{10,26},{12,28},{14,30},{16,0},... | collective-permute-start | bytes 1990664 | tf_op jit(solution)/shard_map/ppermute | solution.py:77
  45.4 47.3 %collective-permute-start.9 = (bf16[224,1152]{1,0:T(8,128)(2,1)S(1)}, bf16[224,1152]{1,0:T(8,128)(2,1)S(1)}, u32[]{:S(2)}, u32[]{:S(2)}) collective-permute-start(bf16[224,1152]{1,0:T(8,128)(2,1)S(1)} %fusion.73), channel_id=1, source_target_pairs={{0,16},{2,18},{4,20},{6,22},{8,24},{10,26},{12,28},{14,30},{16,0},... | collective-permute-start | bytes 1548296 | tf_op jit(solution)/shard_map/ppermute | solution.py:77
  51.8 3.8 %copy-start.1 = (bf16[512,1152]{1,0:T(8,128)(2,1)S(1)}, bf16[512,1152]{1,0:T(8,128)(2,1)}, u32[]{:S(2)}) copy-start(bf16[512,1152]{1,0:T(8,128)(2,1)} %refs_0_) | copy-start | bytes 3538948
  51.8 17.1 %collective-permute-start.5 = (bf16[512,1152]{1,0:T(8,128)(2,1)S(1)}, bf16[512,1152]{1,0:T(8,128)(2,1)S(1)}, u32[]{:S(2)}, u32[]{:S(2)}) collective-permute-start(bf16[512,1152]{1,0:T(8,128)(2,1)S(1)} %convolution_convert_fusion.2), channel_id=1, source_target_pairs={{0,2},{2,0},{4,6},{6,4},{8,10},{10,8},{12,14},{14,12},{16,18},{18,... | collective-permute-start | bytes 3538952 | tf_op jit(solution)/shard_map/ppermute | solution.py:77
  51.9 28.5 %collective-permute-start.8 = (bf16[512,1152]{1,0:T(8,128)(2,1)S(1)}, bf16[512,1152]{1,0:T(8,128)(2,1)S(1)}, u32[]{:S(2)}, u32[]{:S(2)}) collective-permute-start(bf16[512,1152]{1,0:T(8,128)(2,1)S(1)} %convolution_convert_fusion), channel_id=1, source_target_pairs={{0,4},{2,6},{4,0},{6,2},{8,12},{10,14},{12,8},{14,10},{16,20},{18,... | collective-permute-start | bytes 3538952 | tf_op jit(solution)/shard_map/ppermute | solution.py:77
  53.8 28.0 %collective-permute-start.7 = (bf16[512,1152]{1,0:T(8,128)(2,1)S(1)}, bf16[512,1152]{1,0:T(8,128)(2,1)S(1)}, u32[]{:S(2)}, u32[]{:S(2)}) collective-permute-start(bf16[512,1152]{1,0:T(8,128)(2,1)S(1)} %convolution_convert_fusion.1), channel_id=1, source_target_pairs={{0,1},{1,0},{2,3},{3,2},{4,5},{5,4},{6,7},{7,6},{8,9},{9,8},{10,11... | collective-permute-start | bytes 3538952 | tf_op jit(solution)/shard_map/ppermute | solution.py:77
  70.9 28.0 %collective-permute-start.6 = (bf16[128,1152]{1,0:T(8,128)(2,1)S(1)}, bf16[128,1152]{1,0:T(8,128)(2,1)S(1)}, u32[]{:S(2)}, u32[]{:S(2)}) collective-permute-start(bf16[128,1152]{1,0:T(8,128)(2,1)S(1)} %get-tuple-element.43), channel_id=1, source_target_pairs={{0,16},{2,18},{4,20},{6,22},{8,24},{10,26},{12,28},{14,30},{16,0},... | collective-permute-start | bytes 884744 | tf_op jit(solution)/shard_map/ppermute | solution.py:77
  71.0 34.2 %collective-permute-start.10 = (bf16[128,1152]{1,0:T(8,128)(2,1)S(1)}, bf16[128,1152]{1,0:T(8,128)(2,1)S(1)}, u32[]{:S(2)}, u32[]{:S(2)}) collective-permute-start(bf16[128,1152]{1,0:T(8,128)(2,1)S(1)} %get-tuple-element.42), channel_id=1, source_target_pairs={{0,16},{2,18},{4,20},{6,22},{8,24},{10,26},{12,28},{14,30},{16,0},... | collective-permute-start | bytes 884744 | tf_op jit(solution)/shard_map/ppermute | solution.py:77
  92.7 13.5 %collective-permute-start.11 = (bf16[32,1152]{1,0:T(8,128)(2,1)S(1)}, bf16[32,1152]{1,0:T(8,128)(2,1)S(1)}, u32[]{:S(2)}, u32[]{:S(2)}) collective-permute-start(bf16[32,1152]{1,0:T(8,128)(2,1)S(1)} %slice.24), channel_id=1, source_target_pairs={{0,16},{2,18},{4,20},{6,22},{16,0},{18,2},{20,4},{22,6},{1,17},{3,... | collective-permute-start | bytes 221192 | tf_op jit(solution)/shard_map/ppermute | solution.py:77
  99.0 7.2 %collective-permute-start.12 = (bf16[32,1152]{1,0:T(8,128)(2,1)S(1)}, bf16[32,1152]{1,0:T(8,128)(2,1)S(1)}, u32[]{:S(2)}, u32[]{:S(2)}) collective-permute-start(bf16[32,1152]{1,0:T(8,128)(2,1)S(1)} %slice.24), channel_id=1, source_target_pairs={{8,24},{10,26},{12,28},{14,30},{24,8},{26,10},{28,12},{30,14},{9,2... | collective-permute-start | bytes 221192 | tf_op jit(solution)/shard_map/ppermute | solution.py:77
